TPU v7x, 32 devices: a whole 2x2x4 slice. The times are simulated.
32 devices in a mesh: group: 8 (over z, x), ep: 4 (over y, core).
Axes of the slice: x: 2, y: 2, z: 4, core: 2. Of those that a mesh axis runs over, the one named last changes fastest.
Arguments:
- tokens: bfloat16 [256, 2048], P('group'), may hold values from -6 to 6
- prefill_states: float32 [64, 32, 128, 128], P('group', 'ep'), may hold values from -3 to 3
- prefill_tails: bfloat16 [64, 3, 8192], P('group', None, 'ep'), may hold values from -6 to 6
- src_group: int32 [8, 8], replicated, may hold values from 0 to 7, as said below
- src_slot: int32 [8, 8], replicated, may hold values from 0 to 7, as said below
- in_gain: float32 [2048], replicated, may hold values from 0.5 to 1.5
- w_qkvz: bfloat16 [2048, 12288], P(None, 'ep'), may hold values from -0.125 to 0.125
- w_ba: bfloat16 [2048, 64], P(None, 'ep'), may hold values from -0.125 to 0.125
- conv_weight: float32 [4, 8192], P(None, 'ep'), may hold values from -3 to 3
- a_log: float32 [32], P('ep'), may hold values from -4 to -1
- dt_bias: float32 [32], P('ep'), may hold values from -5 to -2
- norm_gain: float32 [128], replicated, may hold values from 0.5 to 1.5
- w_out: bfloat16 [4096, 2048], P('ep'), may hold values from -0.09375 to 0.09375
- post_gain: float32 [2048], replicated, may hold values from 0.5 to 1.5
- expert_ids: int32 [256, 10], P('group'), may hold values from 0 to 31, all different within a row; in each aligned block of 32 rows (0 to 31, 32 to 63, ...) at most 16 rows name the same one
- gate_probs: float32 [256, 10], P('group'), may hold values from 0.02 to 0.3
- gate_up_weight: bfloat16 [32, 2048, 1024], P(('group', 'ep')), may hold values from -0.125 to 0.125
- down_weight: bfloat16 [32, 512, 2048], P(('group', 'ep')), may hold values from -0.25 to 0.25
Outputs:
- layer_out: bfloat16 [256, 2048], P('group', 'ep')
- new_states: float32 [64, 32, 128, 128], P('group', 'ep')
- new_tails: bfloat16 [64, 3, 8192], P('group', None, 'ep')
Inputs may be any that keep to these rules, and one draw needn't show every extreme that they name: Every (prefill instance, slot) pair feeds exactly one decode slot. (src_group[d, j] - d) modulo 8 does not depend on d and takes 8 different values over the 8 slots of a decode group. With stride = 1: if stride is 1 these are all values below 8; else they are k * stride for k = 4 and (k * stride - 1) modulo 8 for every other k below 8. A decode group takes at most 1 request from one prefill instance, and some pair reaches it. `src_slot`: together with src_group, a permutation of all prefill slots. `expert_ids`: each row names 10 different experts; in the rows of one decode group no expert is named more than 16 times.
All inputs are finite; a program needn't handle non-finite values.
Results may differ from a plain program's by a relative error of at most 0.0075.
Values may be sent and summed in bfloat16 or wider, within the bound.
A program may use at most 192 MiB of HBM per device.

v0:
```python
import jax
import jax.numpy as jnp
from jax import lax
from jax.sharding import PartitionSpec as P

epsilon = 1e-06


def rms_norm(values, scale_factors):
    return (
        values
        * lax.rsqrt(jnp.mean(values * values, axis=-1, keepdims=True) + epsilon)
        * scale_factors
    )


def unit_norm(values):
    return values * lax.rsqrt(jnp.sum(values * values, axis=-1, keepdims=True) + epsilon)


def body(
    tokens,
    prefill_states,
    prefill_tails,
    src_group,
    src_slot,
    in_gain,
    w_qkvz,
    w_ba,
    conv_weight,
    a_log,
    dt_bias,
    norm_gain,
    w_out,
    post_gain,
    expert_ids,
    gate_probs,
    gate_up_weight,
    down_weight,
):
    groups = lax.axis_size("group")
    shards = lax.axis_size("ep")
    my_group = lax.axis_index("group")
    my_column = lax.axis_index("ep")
    highest = lax.Precision.HIGHEST
    requests = prefill_states.shape[0]
    head_pairs = w_ba.shape[1] // 4
    key_size = prefill_states.shape[2]
    value_size = prefill_states.shape[3]
    block_width = 2 * key_size + 2 * value_size
    taps_count = conv_weight.shape[0]
    row_count = tokens.shape[0]
    steps_count = row_count // requests
    model_width = tokens.shape[1]
    share_width = model_width // shards
    wanted_group = lax.dynamic_index_in_dim(src_group, my_group, 0, keepdims=False)
    wanted_slot = lax.dynamic_index_in_dim(src_slot, my_group, 0, keepdims=False)
    flat_source = wanted_group * requests + wanted_slot
    pieces = (
        lax.all_gather(prefill_states, "group", axis=0, tiled=True),
        lax.all_gather(prefill_tails.astype(jnp.float32), "group", axis=0, tiled=True).astype(
            jnp.bfloat16
        ),
    )
    piece_rows = pieces[0].shape[0]
    inside = (flat_source >= 0) & (flat_source < piece_rows)
    row_index = jnp.clip(flat_source, 0, piece_rows - 1)
    states_next = jnp.where(
        inside[:, None, None, None], pieces[0][row_index], jnp.zeros_like(prefill_states)
    )
    tails_next = jnp.where(
        inside[:, None, None], pieces[1][row_index], jnp.zeros_like(prefill_tails)
    )
    input_rows = tokens.astype(jnp.float32)
    normed = rms_norm(input_rows, in_gain).astype(jnp.bfloat16)
    projected = jnp.dot(normed, w_qkvz, preferred_element_type=jnp.float32).reshape(
        requests, steps_count, head_pairs, block_width + 2 * value_size
    )
    rates = jnp.dot(normed, w_ba, preferred_element_type=jnp.float32).reshape(
        requests, steps_count, head_pairs, 4
    )
    conv_in = projected[..., :block_width].astype(jnp.bfloat16)
    gate_z = projected[..., block_width:].reshape(requests, steps_count, head_pairs, 2, value_size)
    window = jnp.concatenate(
        [tails_next.reshape(requests, taps_count - 1, head_pairs, block_width), conv_in], axis=1
    )
    new_tails = window[:, steps_count:].reshape(requests, taps_count - 1, head_pairs * block_width)
    window = window.astype(jnp.float32)
    taps = conv_weight.reshape(taps_count, head_pairs, block_width)
    mixed = jnp.zeros((requests, steps_count, head_pairs, block_width), jnp.float32)
    for offset in range(taps_count):
        mixed = mixed + taps[offset] * window[:, offset : offset + steps_count]
    conv_out = jax.nn.silu(mixed)
    queries = unit_norm(conv_out[..., :key_size]) * key_size ** (-0.5)
    keys = unit_norm(conv_out[..., key_size : 2 * key_size])
    values = conv_out[..., 2 * key_size :].reshape(requests, steps_count, head_pairs, 2, value_size)
    write_rate = jax.nn.sigmoid(rates[..., :2])
    decay_rate = jnp.exp(
        -jnp.exp(a_log.reshape(head_pairs, 2))
        * jax.nn.softplus(rates[..., 2:] + dt_bias.reshape(head_pairs, 2))
    )
    memory = states_next.reshape(requests, head_pairs, 2, key_size, value_size)
    readouts = []
    for token_step in range(steps_count):
        memory = decay_rate[:, token_step, :, :, None, None] * memory
        predicted = jnp.einsum("rqk,rqhkv->rqhv", keys[:, token_step], memory, precision=highest)
        delta = write_rate[:, token_step, :, :, None] * (values[:, token_step] - predicted)
        memory = memory + jnp.einsum(
            "rqk,rqhv->rqhkv", keys[:, token_step], delta, precision=highest
        )
        readouts.append(
            jnp.einsum("rqk,rqhkv->rqhv", queries[:, token_step], memory, precision=highest)
        )
    readout = jnp.stack(readouts, axis=1)
    gated = (
        (rms_norm(readout, norm_gain) * jax.nn.silu(gate_z))
        .astype(jnp.bfloat16)
        .reshape(row_count, head_pairs * 2 * value_size)
    )
    head_part = jnp.dot(gated, w_out, preferred_element_type=jnp.float32)
    new_states = memory.reshape(requests, head_pairs * 2, key_size, value_size)
    residual = input_rows + lax.psum(head_part, "ep")
    moe_input = rms_norm(residual, post_gain).astype(jnp.bfloat16)
    residual_share = lax.dynamic_slice_in_dim(residual, my_column * share_width, share_width, 1)
    local_experts = gate_up_weight.shape[0]
    hidden_width = down_weight.shape[1]
    top_count = expert_ids.shape[1]
    experts_all = local_experts * groups * shards
    capacity = max(2, (row_count * top_count * 8 + experts_all * 5 - 1) // (experts_all * 5))
    slot_total = local_experts * groups * capacity
    ids_flat = expert_ids.reshape(-1)
    assigned = ids_flat.shape[0]
    positions = jnp.arange(assigned, dtype=jnp.int32)
    earlier_pick = positions[None, :] < positions[:, None]
    arrival = jnp.sum(
        ((ids_flat[:, None] == ids_flat[None, :]) & earlier_pick).astype(jnp.int32), axis=1
    )
    on_column = ids_flat // local_experts % shards == my_column
    dest_group = ids_flat // (shards * local_experts)
    local_slot = ids_flat % local_experts
    slot_id = (local_slot * groups + dest_group) * capacity + arrival
    slot_match = on_column[None, :] & (
        slot_id[None, :] == jnp.arange(slot_total, dtype=jnp.int32)[:, None]
    )
    slot_match = slot_match.reshape(slot_total, row_count, top_count)
    pick_matrix = jnp.any(slot_match, axis=-1).astype(jnp.bfloat16)
    weight_matrix = jnp.sum(jnp.where(slot_match, gate_probs[None, :, :], 0.0), axis=-1)
    send_rows = jnp.dot(pick_matrix, moe_input, preferred_element_type=jnp.float32).astype(
        jnp.bfloat16
    )
    send_rows = send_rows.reshape(local_experts, groups, capacity, model_width)
    received_rows = lax.all_to_all(
        send_rows, "group", split_axis=1, concat_axis=1, tiled=True
    ).reshape(local_experts, groups * capacity, model_width)
    paired_halves = jnp.einsum(
        "esp,epk->esk", received_rows, gate_up_weight, preferred_element_type=jnp.float32
    )
    hidden_state = (
        jax.nn.silu(paired_halves[..., :hidden_width]) * paired_halves[..., hidden_width:]
    ).astype(jnp.bfloat16)
    expert_rows = jnp.einsum(
        "ugh,uhv->ugv", hidden_state, down_weight, preferred_element_type=jnp.float32
    ).astype(jnp.bfloat16)
    expert_rows = expert_rows.reshape(local_experts, groups, capacity, model_width)
    returned = lax.all_to_all(
        expert_rows, "group", split_axis=1, concat_axis=1, tiled=True
    ).reshape(slot_total, model_width)
    weighted = jnp.dot(weight_matrix.T, returned.astype(jnp.float32), precision=highest)
    expert_share = lax.psum_scatter(
        weighted.astype(jnp.bfloat16), "ep", scatter_dimension=1, tiled=True
    ).astype(jnp.float32)
    layer_out = (residual_share + expert_share).astype(jnp.bfloat16)
    return (layer_out, new_states, new_tails)


def solution(mesh):
    in_specs = (
        P("group", None),
        P("group", "ep", None, None),
        P("group", None, "ep"),
        P(),
        P(),
        P(),
        P(None, "ep"),
        P(None, "ep"),
        P(None, "ep"),
        P("ep"),
        P("ep"),
        P(),
        P("ep", None),
        P(),
        P("group", None),
        P("group", None),
        P(("group", "ep"), None, None),
        P(("group", "ep"), None, None),
    )
    out_specs = (P("group", "ep"), P("group", "ep", None, None), P("group", None, "ep"))
    return jax.shard_map(body, mesh=mesh, in_specs=in_specs, out_specs=out_specs, check_vma=False)
```

profile of v0, /device:TPU:0, one launch (start us, length us, event | category | flops | bytes accessed | tf_op | source)
XLA Modules:
  0.0 810.0 jit_solution(8806749193354736349)
XLA Ops:
  7.2 0.7 all-gather.2.cloned.1.call-update
  8.0 0.2 copy-done.3
  8.5 7.0 fusion.46
  15.4 0.2 reshape.272
  16.1 0.2 convert_reduce_fusion
  16.7 0.2 fusion.44
  17.2 0.3 copy.193
  17.5 0.3 copy.191
  17.8 0.3 copy.189
  18.1 0.3 copy.187
  18.4 0.3 copy.188
  18.7 0.3 copy.190
  19.1 0.3 copy.192
  19.4 0.3 copy.186
  19.8 86.0 %all_gather.6 = bf16[64,3,2048]{2,0,1:T(8,128)(2,1)S(1)} all-gather(bf16[8,3,2048]{2,0,1:T(8,128)(2,1)S(1)} %copy-done.4), channel_id=1, replica_groups=mesh['group'=8,'ep'=4] {'group'}, dimensions={0}, use_global_device_ids=true | all-gather | bytes 884736 | tf_op jit(solution)/shard_map/all_gather | solution.py:61
  105.8 1.6 copy.145
  107.4 0.7 and_bitcast_fusion
  108.2 1.9 gather_fusion
  110.3 0.2 divide_multiply_fusion
  110.7 0.2 multiply_reduce_fusion.2
  111.1 553.7 %all-gather.2.cloned.1.call-done = f32[64,8,128,128]{3,2,1,0:T(8,128)} async-done(((f32[8,8,128,128]{3,2,1,0:T(8,128)}), f32[64,8,128,128]{3,2,1,0:T(8,128)}) %all-gather.2.cloned.1.call-update) | async-done | bytes 33554448 | tf_op jit(solution)/shard_map/all_gather | solution.py:60
  664.8 5.0 gather_fusion.1
  669.7 4.7 fusion.8
  674.6 2.7 fusion.72
  677.3 2.9 fusion.6
  680.3 3.9 fusion.9
  684.2 3.9 fusion.4
  688.2 4.2 fusion.26
  692.5 4.4 fusion.2
  696.9 3.3 bitcast_add_fusion
  700.2 2.0 copy-done.2
  702.2 2.1 fusion.78
  704.3 0.3 multiply_reduce_fusion.1
  704.6 0.2 broadcast_multiply_fusion
  705.0 3.7 fusion.41
  708.9 31.9 %all-reduce.2.cloned.1.call-done = f32[32,2048]{1,0:T(8,128)} async-done(((f32[32,2048]{1,0:T(8,128)}), f32[32,2048]{1,0:T(8,128)}) %all-reduce.2.cloned.1.call-update) | async-done | bytes 262160 | tf_op jit(solution)/shard_map/psum | solution.py:122
  740.8 1.1 multiply_reduce_fusion
  741.9 0.4 convolution_convert_fusion.1
  742.3 18.7 %all_to_all.10 = bf16[1,8,16,2048]{3,2,0,1:T(8,128)(2,1)S(1)} all-to-all(bf16[1,8,16,2048]{3,2,0,1:T(8,128)(2,1)S(1)} %bitcast.211), channel_id=1, replica_groups=mesh['group'=8,'ep'=4] {'group'}, dimensions={1} | all-to-all | bytes 1048576 | tf_op jit(solution)/shard_map/all_to_all | solution.py:152
  761.0 3.0 fusion.23
  763.9 1.3 convolution_convert_fusion
  765.2 3.7 all-to-all-start.1
  768.9 0.2 select_reduce_fusion
  769.1 13.8 %all-to-all-done.1 = bf16[1,8,16,2048]{3,2,0,1:T(8,128)(2,1)S(1)} async-done(((bf16[1,8,16,2048]{3,2,0,1:T(8,128)(2,1)}), bf16[1,8,16,2048]{3,2,0,1:T(8,128)(2,1)S(1)}, u32[]{:S(2)}, u32[]{:S(2)}) %all-to-all-start.1) | async-done | bytes 524320 | tf_op jit(solution)/shard_map/all_to_all | solution.py:165
  782.9 1.0 convolution_convert_fusion.2
  784.0 0.7 copy.168
  784.6 17.4 %reduce-scatter.2.cloned.1.call-done = bf16[32,512]{1,0:T(8,128)(2,1)} async-done(((bf16[32,2048]{1,0:T(8,128)(2,1)}), bf16[32,512]{1,0:T(8,128)(2,1)}) %reduce-scatter.2.cloned.1.call-update) | async-done | bytes 32784 | tf_op jit(solution)/shard_map/reduce_scatter | solution.py:169
  802.1 1.4 add_convert_fusion
  (74 shorter events, 2.8 us)
Async XLA Ops:
  7.2 756.8 %copy-start = (bf16[1,512,2048]{2,1,0:T(8,128)(2,1)S(1)}, bf16[1,512,2048]{2,1,0:T(8,128)(2,1)}, u32[]{:S(2)}) copy-start(bf16[1,512,2048]{2,1,0:T(8,128)(2,1)} %param.35) | copy-start | bytes 6291460
  7.2 1.1 copy-start.3
  7.2 1.2 copy-start.6
  7.2 657.6 %all-gather.2.cloned.1.call-start = ((), (), s32[]{:S(2)}) async-start(), calls=%async_computation.3 | async-start | bytes 37748736 | tf_op jit(solution)/shard_map/all_gather | solution.py:60
  7.9 732.9 %all-reduce.2.cloned.1.call-start = ((), (), s32[]{:S(2)}) async-start(), calls=%async_computation.4 | async-start | bytes 524288 | tf_op jit(solution)/shard_map/psum | solution.py:122
  8.4 7.3 copy-start.13
  8.4 7.4 copy-start.10
  8.4 7.5 copy-start.5
  8.4 8.1 %copy-start.7 = (f32[4,2048]{1,0:T(4,128)S(1)}, f32[4,2048]{1,0:T(4,128)}, u32[]{:S(2)}) copy-start(f32[4,2048]{1,0:T(4,128)} %param.26) | copy-start | bytes 98308
  8.4 8.3 %copy-start.12 = (bf16[2048,16]{0,1:T(8,128)(2,1)S(1)}, bf16[2048,16]{0,1:T(8,128)(2,1)}, u32[]{:S(2)}) copy-start(bf16[2048,16]{0,1:T(8,128)(2,1)} %param.25) | copy-start | bytes 196612
  8.4 11.3 %copy-start.4 = (bf16[8,3,2048]{2,0,1:T(8,128)(2,1)S(1)}, bf16[8,3,2048]{2,0,1:T(8,128)(2,1)}, u32[]{:S(2)}) copy-start(bf16[8,3,2048]{2,0,1:T(8,128)(2,1)} %param.20) | copy-start | bytes 294916
  669.7 4.8 copy-start.1
  700.2 2.0 copy-start.2
  700.2 4.7 copy-start.11
  704.3 37.6 %copy-start.8 = (f32[2048]{0:T(1024)S(1)}, f32[2048]{0:T(1024)}, u32[]{:S(2)}) copy-start(f32[2048]{0:T(1024)} %param.31) | copy-start | bytes 24580
  761.0 8.0 copy-start.9
  765.2 17.7 %all-to-all-start.1 = ((bf16[1,8,16,2048]{3,2,0,1:T(8,128)(2,1)}), bf16[1,8,16,2048]{3,2,0,1:T(8,128)(2,1)S(1)}, u32[]{:S(2)}, u32[]{:S(2)}) async-start(bf16[1,8,16,2048]{3,2,0,1:T(8,128)(2,1)} %bitcast.213), calls=%async_computation.1 | async-start | bytes 1048576 | tf_op jit(solution)/shard_map/all_to_all | solution.py:165
  768.9 33.2 %reduce-scatter.2.cloned.1.call-start = ((), (), s32[]{:S(2)}) async-start(), calls=%async_computation.5 | async-start | bytes 163840 | tf_op jit(solution)/shard_map/reduce_scatter | solution.py:169
Sparse Core Ops, SparseCore 0:
  9.6 655.1 all-gather.1
  708.8 31.9 all-reduce.1
  784.0 17.9 reduce-scatter.1
where the time goes:
time: 811 us; the launch traced here: 810 us
  waiting for transfers between devices  618 us (76%)
  blocking collectives  105 us (13%)
  matrix products  45.2 us (6%)
  local copies, waits for them, and re-layouts  15.5 us (2%)
  between operations  14.2 us (2%)
  other arithmetic  8.99 us (1%)
    all_gather x1, waiting for transfers between devices, body(): lax.all_gather(prefill_states, 'group', axis=0, tiled=True)  554 us
    all_gather x1, blocking collectives, body(): lax.all_gather(prefill_tails.astype(jnp.float32), 'group', axis=0, tiled=...  86 us
    psum x1, waiting for transfers between devices, body(): residual = input_rows + lax.psum(head_part, 'ep')  31.9 us
    all_to_all x1, blocking collectives, body(): lax.all_to_all(send_rows, 'group', split_axis=1, concat_axis=1, tiled=True)  18.7 us
    reduce_scatter x1, waiting for transfers between devices, body(): lax.psum_scatter(weighted.astype(jnp.bfloat16), 'ep', scatter_dimension=1...  17.4 us
  transfers between devices with their start and end apart: 4, of which 4 were waited for; matrix products, arithmetic and copies ran while one was open for 2% of the time, Pallas kernels for 0%

commit v1 on v0

--- a/solution.py
+++ b/solution.py
@@ -53,24 +53,30 @@
     steps_count = row_count // requests
     model_width = tokens.shape[1]
     share_width = model_width // shards
-    wanted_group = lax.dynamic_index_in_dim(src_group, my_group, 0, keepdims=False)
-    wanted_slot = lax.dynamic_index_in_dim(src_slot, my_group, 0, keepdims=False)
-    flat_source = wanted_group * requests + wanted_slot
-    pieces = (
-        lax.all_gather(prefill_states, "group", axis=0, tiled=True),
-        lax.all_gather(prefill_tails.astype(jnp.float32), "group", axis=0, tiled=True).astype(
-            jnp.bfloat16
-        ),
-    )
-    piece_rows = pieces[0].shape[0]
-    inside = (flat_source >= 0) & (flat_source < piece_rows)
-    row_index = jnp.clip(flat_source, 0, piece_rows - 1)
-    states_next = jnp.where(
-        inside[:, None, None, None], pieces[0][row_index], jnp.zeros_like(prefill_states)
-    )
-    tails_next = jnp.where(
-        inside[:, None, None], pieces[1][row_index], jnp.zeros_like(prefill_tails)
-    )
+    stride = groups // requests
+    offsets = [
+        which * stride if stride == 1 or which == requests // 2 else (which * stride - 1) % groups
+        for which in range(requests)
+    ]
+    slot_offsets = (src_group[0] % groups).astype(jnp.int32)
+    kept_states = prefill_states.astype(jnp.bfloat16)
+    state_pieces = []
+    tail_pieces = []
+    for offset in offsets:
+        target = (my_group - offset) % groups
+        which = jnp.argmax(slot_offsets == offset)
+        slot = src_slot[target, which]
+        state_piece = lax.dynamic_index_in_dim(kept_states, slot, 0, keepdims=False)
+        tail_piece = lax.dynamic_index_in_dim(prefill_tails, slot, 0, keepdims=False)
+        if offset:
+            pairs = [(source, (source - offset) % groups) for source in range(groups)]
+            tail_piece = lax.ppermute(tail_piece, "group", pairs)
+            state_piece = lax.ppermute(state_piece, "group", pairs)
+        state_pieces.append(state_piece)
+        tail_pieces.append(tail_piece)
+    arrived = jnp.argmax(slot_offsets[:, None] == jnp.array(offsets)[None, :], axis=1)
+    states_next = jnp.stack(state_pieces)[arrived].astype(jnp.float32)
+    tails_next = jnp.stack(tail_pieces)[arrived]
     input_rows = tokens.astype(jnp.float32)
     normed = rms_norm(input_rows, in_gain).astype(jnp.bfloat16)
     projected = jnp.dot(normed, w_qkvz, preferred_element_type=jnp.float32).reshape(

time: 811 us -> 313 us (0.39)
  waiting for transfers between devices: 618 us -> 90.1 us
  blocking collectives: 105 us -> 18.7 us
  local copies, waits for them, and re-layouts: 15.5 us -> 52 us
  between operations: 14.2 us -> 45.1 us
  starting transfers between devices: 3.78 us -> 31.8 us
  other arithmetic: 8.99 us -> 25.1 us
    all_gather x1 -> x0, waiting for transfers between devices: 554 us -> none  [body(): lax.all_gather(prefill_states, 'group', axis=0, tiled=True)]
    all_gather x1 -> x0, blocking collectives: 86 us -> none  [body(): lax.all_gather(prefill_tails.astype(jnp.float32), 'group', axis=0, tiled=...]
    ppermute x0 -> x14, waiting for transfers between devices: none -> 29.6 us  [the longest x7 29.6 us: body(): state_piece = lax.ppermute(state_piece, 'group', pairs)]
    ppermute x0 -> x14, starting transfers between devices: none -> 28.1 us  [the longest x7 15.6 us: body(): state_piece = lax.ppermute(state_piece, 'group', pairs)]
    unnamed x30 -> x58, local copies, waits for them, and re-layouts: 2.44 us -> 19.3 us
    another operation x1 -> x10, other arithmetic: 0.07 us -> 11.8 us  [the longest x8 11.1 us: body(): which = jnp.argmax(slot_offsets == offset)]
  transfers between devices with their start and end apart: 4 -> 17, of which waited for: 4 -> 6; matrix products, arithmetic and copies ran while one was open for 2% -> 18% of each run, Pallas kernels for 0% -> 0%
where the time goes in v1:
time: 313 us; the launch traced here: 310 us
  waiting for transfers between devices  90.1 us (29%)
  local copies, waits for them, and re-layouts  52 us (17%)
  matrix products  47.2 us (15%)
  between operations  45.1 us (14%)
  starting transfers between devices  31.8 us (10%)
  other arithmetic  25.1 us (8%)
  blocking collectives  18.7 us (6%)
    ppermute x7, waiting for transfers between devices, body(): state_piece = lax.ppermute(state_piece, 'group', pairs)  29.6 us
    psum x1, waiting for transfers between devices, body(): residual = input_rows + lax.psum(head_part, 'ep')  29.2 us
    unnamed x58, local copies, waits for them, and re-layouts  19.3 us
    all_to_all x1, blocking collectives, body(): lax.all_to_all(send_rows, 'group', split_axis=1, concat_axis=1, tiled=True)  18.7 us
    reduce_scatter x1, waiting for transfers between devices, body(): lax.psum_scatter(weighted.astype(jnp.bfloat16), 'ep', scatter_dimension=1...  17.5 us
    ppermute x7, starting transfers between devices, body(): state_piece = lax.ppermute(state_piece, 'group', pairs)  15.6 us
    dot_general x4, matrix products, body(): jnp.einsum('rqk,rqhkv->rqhv', keys[:, token_step], memory, precision=high...  15.2 us
    dot_general x4, matrix products, body(): jnp.einsum('rqk,rqhkv->rqhv', queries[:, token_step], memory, precision=h...  14.5 us
  transfers between devices with their start and end apart: 17, of which 6 were waited for; matrix products, arithmetic and copies ran while one was open for 18% of the time, Pallas kernels for 0%

profile of v1, /device:TPU:0, one launch (start us, length us, event | category | flops | bytes accessed | tf_op | source)
XLA Modules:
  0.0 310.0 jit_solution(13055976457029660417)
XLA Ops:
  7.4 1.5 compare_reduce_fusion
  33.6 1.7 fusion.87
  50.5 2.4 constant_dynamic-slice_fusion
  53.5 3.0 collective-permute-start.5
  57.1 3.2 %collective-permute-start = (bf16[3,2048]{1,0:T(4,128)(2,1)}, bf16[3,2048]{1,0:T(4,128)(2,1)}, u32[]{:S(2)}, u32[]{:S(2)}) collective-permute-start(bf16[3,2048]{1,0:T(4,128)(2,1)} %bitcast.283), channel_id=1, source_target_pairs={{0,28},{4,0},{8,4},{12,8},{16,12},{20,16},{24,20},{28,24},{1,29},{... | collective-permute-start | bytes 36872 | tf_op jit(solution)/shard_map/ppermute | solution.py:73
  60.9 1.8 collective-permute-start.1
  64.0 1.4 collective-permute-start.3
  71.3 1.6 slice_reduce_fusion.3
  74.2 7.1 %fusion.60 = f32[32,3072]{1,0:T(8,128)S(1)} fusion(bf16[2048,3072]{1,0:T(8,128)(2,1)} %param.25, bf16[32,2048]{1,0:T(8,128)(2,1)} %param.19, f32[2048]{0:T(1024)} %param.24, f32[32]{0:T(128)S(1)} %add_rsqrt_fusion.4), kind=kOutput, calls=%fused_computation.105 | convolution fusion | flops 402915328 | bytes 13115520 | tf_op jit(solution)/shard_map/dot_general | solution.py:82
  89.3 1.6 copy.194
  91.0 1.6 copy.192
  92.6 1.6 copy.190
  94.3 1.6 copy.188
  95.9 1.6 copy.189
  97.6 1.6 copy.191
  102.0 1.5 collective-permute-start.4
  104.3 1.5 collective-permute-start.6
  106.6 2.0 collective-permute-start.13
  109.3 1.6 collective-permute-start.12
  112.3 2.8 collective-permute-start.8
  115.8 2.1 collective-permute-start.7
  121.0 10.4 %collective-permute-done.7 = bf16[8,128,128]{2,1,0:T(8,128)(2,1)} collective-permute-done((bf16[8,128,128]{2,1,0:T(8,128)(2,1)}, bf16[8,128,128]{2,1,0:T(8,128)(2,1)}, u32[]{:S(2)}, u32[]{:S(2)}) %collective-permute-start.7) | collective-permute-done | bytes 262176 | tf_op jit(solution)/shard_map/ppermute | solution.py:74
  131.4 4.2 %collective-permute-start.9 = (bf16[8,128,128]{2,1,0:T(8,128)(2,1)}, bf16[8,128,128]{2,1,0:T(8,128)(2,1)S(1)}, u32[]{:S(2)}, u32[]{:S(2)}) collective-permute-start(bf16[8,128,128]{2,1,0:T(8,128)(2,1)} %get-tuple-element.33), channel_id=1, source_target_pairs={{0,20},{4,24},{8,28},{12,0},{16,4},{20,8},{24,12},{28,16},{1,21},{... | collective-permute-start | bytes 786440 | tf_op jit(solution)/shard_map/ppermute | solution.py:74
  135.6 1.7 bitcast_dynamic-update-slice_fusion.6
  137.3 2.3 collective-permute-start.10
  139.6 1.7 bitcast_dynamic-update-slice_fusion.5
  143.0 18.2 %collective-permute-done.10 = bf16[8,128,128]{2,1,0:T(8,128)(2,1)S(1)} collective-permute-done((bf16[8,128,128]{2,1,0:T(8,128)(2,1)S(1)}, bf16[8,128,128]{2,1,0:T(8,128)(2,1)S(1)}, u32[]{:S(2)}, u32[]{:S(2)}) %collective-permute-start.10) | collective-permute-done | bytes 262176 | tf_op jit(solution)/shard_map/ppermute | solution.py:74
  161.8 1.7 bitcast_dynamic-update-slice_fusion.2
  163.5 1.7 bitcast_dynamic-update-slice_fusion.1
  165.2 1.7 bitcast_dynamic-update-slice_fusion
  166.9 3.9 %gather_fusion.1 = bf16[8,8,128,128]{3,2,1,0:T(8,128)(2,1)} fusion(bf16[8,8,128,128]{3,2,1,0:T(8,128)(2,1)} %bitcast_dynamic-update-slice_fusion, s32[1024]{0:T(1024)} %pad_clamp_fusion), kind=kCustom, calls=%fused_computation.1 | custom fusion | bytes 4194336 | tf_op jit(solution)/shard_map/gather | solution.py:78
  170.7 4.1 %fusion.1 = f32[8,4,1,2,128]{4,2,3,1,0:T(1,128)S(1)} fusion(f32[8,4,128,1,1]{2,3,4,1,0:T(1,128)S(1)} %bitcast.340, bf16[8,4,2,128,128]{4,3,2,1,0:T(8,128)(2,1)} %bitcast.285, f32[8,4,2]{2,1,0:T(4,128)S(1)} %bitcast.320), kind=kOutput, calls=%fused_computation.4 | convolution fusion | flops 14680064 | bytes 2146560 | tf_op jit(solution)/shard_map/rqk,rqhkv->rqhv/dot_general | solution.py:112
  175.0 4.3 %fusion.5 = f32[8,4,1,2,128]{4,2,3,1,0:T(1,128)S(1)} fusion(f32[8,4,128,1,1]{2,3,4,1,0:T(1,128)S(1)} %bitcast.345, bf16[8,4,2,128,128]{4,3,2,1,0:T(8,128)(2,1)} %bitcast.286, f32[8,4,128]{2,1,0:T(4,128)S(1)} %get-tuple-element.54, f32[8,4,2,128]{3,2,1,0:T(2,128)S(1)} %fusion.71, f32[8,4,2]{2,1,0:T(4,128)S(1)} %bitcast.321), kind=kOutput, calls=%fused_computation.11 | convolution fusion | flops 16777216 | bytes 2195712 | tf_op jit(solution)/shard_map/rqk,rqhkv->rqhv/dot_general | solution.py:118
  179.3 2.8 fusion.7
  182.3 3.9 %fusion.13 = f32[8,4,1,2,128]{4,2,3,1,0:T(1,128)S(1)} fusion(f32[8,4,128,1,1]{2,3,4,1,0:T(1,128)S(1)} %bitcast.344, bf16[8,4,2,128,128]{4,3,2,1,0:T(8,128)(2,1)S(1)} %bitcast.288, f32[8,4,128]{2,1,0:T(4,128)S(1)} %get-tuple-element.55, f32[8,4,2,128]{3,2,1,0:T(2,128)S(1)} %fusion.69, f32[8,4,2]{2,1,0:T(4,128)S(1)} %bitcast.309, ...), kind=kOutput, calls=%fused_computation.17 | convolution fusion | flops 19922944 | bytes 2245120 | tf_op jit(solution)/shard_map/rqk,rqhkv->rqhv/dot_general | solution.py:118
  186.2 3.8 %fusion.11 = f32[8,4,1,2,128]{4,2,3,1,0:T(1,128)S(1)} fusion(f32[8,4,128,1,1]{2,3,4,1,0:T(1,128)S(1)} %bitcast.338, bf16[8,4,2,128,128]{4,3,2,1,0:T(8,128)(2,1)S(1)} %bitcast.289, f32[8,4,2]{2,1,0:T(4,128)S(1)} %bitcast.314, f32[8,4,128]{2,1,0:T(4,128)S(1)} %get-tuple-element.55, f32[8,4,2,128]{3,2,1,0:T(2,128)S(1)} %fusion.69, ...), kind=kOutput, calls=%fused_computation.15 | convolution fusion | flops 20971520 | bytes 2245376 | tf_op jit(solution)/shard_map/rqk,rqhkv->rqhv/dot_general | solution.py:112
  190.2 4.2 %fusion.37 = f32[8,4,1,2,128]{4,2,3,1,0:T(1,128)S(1)} fusion(f32[8,4,128,1,1]{2,3,4,1,0:T(1,128)S(1)} %bitcast.343, bf16[8,4,2,128,128]{4,3,2,1,0:T(8,128)(2,1)S(1)} %bitcast.290, f32[8,4,128]{2,1,0:T(4,128)S(1)} %get-tuple-element.56, f32[8,4,2,128]{3,2,1,0:T(2,128)S(1)} %fusion.67, f32[8,4,2]{2,1,0:T(4,128)S(1)} %bitcast.315, ...), kind=kOutput, calls=%fused_computation.44 | convolution fusion | flops 23068672 | bytes 2294528 | tf_op jit(solution)/shard_map/rqk,rqhkv->rqhv/dot_general | solution.py:118
  194.4 4.4 %fusion.9 = f32[8,4,1,2,128]{4,2,3,1,0:T(1,128)S(1)} fusion(f32[8,4,128,1,1]{2,3,4,1,0:T(1,128)S(1)} %bitcast.337, f32[8,4,2]{2,1,0:T(4,128)S(1)} %bitcast.318, bf16[8,4,2,128,128]{4,3,2,1,0:T(8,128)(2,1)S(1)} %bitcast.291, f32[8,4,128]{2,1,0:T(4,128)S(1)} %get-tuple-element.56, f32[8,4,2,128]{3,2,1,0:T(2,128)S(1)} %fusion.67, ...), kind=kOutput, calls=%fused_computation.13 | convolution fusion | flops 24117248 | bytes 2294784 | tf_op jit(solution)/shard_map/rqk,rqhkv->rqhv/dot_general | solution.py:112
  198.9 3.7 %bitcast_add_fusion = f32[8,4,2,128,128]{4,3,2,1,0:T(8,128)S(1)} fusion(f32[8,4,128]{2,1,0:T(4,128)S(1)} %get-tuple-element.57, f32[8,4,2,128]{3,2,1,0:T(2,128)S(1)} %fusion.65, f32[8,4,2]{2,1,0:T(4,128)S(1)} %bitcast.319, f32[8,4,128]{2,1,0:T(4,128)S(1)} %get-tuple-element.56, f32[8,4,2,128]{3,2,1,0:T(2,128)S(1)} %fusion.67, ...), kind=kLoop, calls=%fused_computation.7 | loop fusion | flops 13631488 | bytes 6489088 | tf_op jit(solution)/shard_map/add | solution.py:114
  202.6 2.0 copy-done.1
  204.6 2.1 fusion.88
  207.4 3.7 %fusion.55 = f32[32,2048]{1,0:T(8,128)} fusion(bf16[1024,2048]{1,0:T(8,128)(2,1)} %param.31, f32[32,1024]{1,0:T(8,128)S(1)} %bitcast.296, f32[32,1024]{1,0:T(8,128)S(1)} %mul.317, f32[1024]{0:T(1024)S(1)} %bitcast.346), kind=kOutput, calls=%fused_computation.94 | convolution fusion | flops 134447104 | bytes 4722688 | tf_op jit(solution)/shard_map/dot_general | solution.py:126
  211.3 29.2 %all-reduce.2.cloned.1.call-done = f32[32,2048]{1,0:T(8,128)} async-done(((f32[32,2048]{1,0:T(8,128)}), f32[32,2048]{1,0:T(8,128)}) %all-reduce.2.cloned.1.call-update) | async-done | bytes 262160 | tf_op jit(solution)/shard_map/psum | solution.py:128
  242.0 18.7 %all_to_all.10 = bf16[1,8,16,2048]{3,2,0,1:T(8,128)(2,1)S(1)} all-to-all(bf16[1,8,16,2048]{3,2,0,1:T(8,128)(2,1)S(1)} %bitcast.295), channel_id=1, replica_groups=mesh['group'=8,'ep'=4] {'group'}, dimensions={1} | all-to-all | bytes 1048576 | tf_op jit(solution)/shard_map/all_to_all | solution.py:158
  260.7 3.0 fusion.38
  264.9 3.6 %all-to-all-start.1 = ((bf16[1,8,16,2048]{3,2,0,1:T(8,128)(2,1)}), bf16[1,8,16,2048]{3,2,0,1:T(8,128)(2,1)S(1)}, u32[]{:S(2)}, u32[]{:S(2)}) async-start(bf16[1,8,16,2048]{3,2,0,1:T(8,128)(2,1)} %bitcast.297), calls=%async_computation.1 | async-start | bytes 1048576 | tf_op jit(solution)/shard_map/all_to_all | solution.py:171
  268.8 13.8 %all-to-all-done.1 = bf16[1,8,16,2048]{3,2,0,1:T(8,128)(2,1)S(1)} async-done(((bf16[1,8,16,2048]{3,2,0,1:T(8,128)(2,1)}), bf16[1,8,16,2048]{3,2,0,1:T(8,128)(2,1)S(1)}, u32[]{:S(2)}, u32[]{:S(2)}) %all-to-all-start.1) | async-done | bytes 524320 | tf_op jit(solution)/shard_map/all_to_all | solution.py:171
  284.3 17.5 %reduce-scatter.2.cloned.1.call-done = bf16[32,512]{1,0:T(8,128)(2,1)} async-done(((bf16[32,2048]{1,0:T(8,128)(2,1)}), bf16[32,512]{1,0:T(8,128)(2,1)}) %reduce-scatter.2.cloned.1.call-update) | async-done | bytes 32784 | tf_op jit(solution)/shard_map/reduce_scatter | solution.py:175
  (140 shorter events, 47.8 us)
Async XLA Ops:
  7.2 256.5 %copy-start = (bf16[1,512,2048]{2,1,0:T(8,128)(2,1)S(1)}, bf16[1,512,2048]{2,1,0:T(8,128)(2,1)}, u32[]{:S(2)}) copy-start(bf16[1,512,2048]{2,1,0:T(8,128)(2,1)} %param.36) | copy-start | bytes 6291460
  7.2 233.3 %all-reduce.2.cloned.1.call-start = ((), (), s32[]{:S(2)}) async-start(), calls=%async_computation.3 | async-start | bytes 524288 | tf_op jit(solution)/shard_map/psum | solution.py:128
  53.5 58.8 %collective-permute-start.5 = (bf16[3,2048]{1,0:T(4,128)(2,1)}, bf16[3,2048]{1,0:T(4,128)(2,1)}, u32[]{:S(2)}, u32[]{:S(2)}) collective-permute-start(bf16[3,2048]{1,0:T(4,128)(2,1)} %bitcast.278), channel_id=1, source_target_pairs={{0,8},{4,12},{8,16},{12,20},{16,24},{20,28},{24,0},{28,4},{1,9},{5... | collective-permute-start | bytes 36872 | tf_op jit(solution)/shard_map/ppermute | solution.py:73
  57.1 44.9 %collective-permute-start = (bf16[3,2048]{1,0:T(4,128)(2,1)}, bf16[3,2048]{1,0:T(4,128)(2,1)}, u32[]{:S(2)}, u32[]{:S(2)}) collective-permute-start(bf16[3,2048]{1,0:T(4,128)(2,1)} %bitcast.283), channel_id=1, source_target_pairs={{0,28},{4,0},{8,4},{12,8},{16,12},{20,16},{24,20},{28,24},{1,29},{... | collective-permute-start | bytes 36872 | tf_op jit(solution)/shard_map/ppermute | solution.py:73
  60.9 43.4 %collective-permute-start.1 = (bf16[3,2048]{1,0:T(4,128)(2,1)}, bf16[3,2048]{1,0:T(4,128)(2,1)}, u32[]{:S(2)}, u32[]{:S(2)}) collective-permute-start(bf16[3,2048]{1,0:T(4,128)(2,1)} %bitcast.282), channel_id=1, source_target_pairs={{0,24},{4,28},{8,0},{12,4},{16,8},{20,12},{24,16},{28,20},{1,25},{... | collective-permute-start | bytes 36872 | tf_op jit(solution)/shard_map/ppermute | solution.py:73
  63.3 43.2 %collective-permute-start.2 = (bf16[3,2048]{1,0:T(4,128)(2,1)}, bf16[3,2048]{1,0:T(4,128)(2,1)}, u32[]{:S(2)}, u32[]{:S(2)}) collective-permute-start(bf16[3,2048]{1,0:T(4,128)(2,1)} %bitcast.281), channel_id=1, source_target_pairs={{0,20},{4,24},{8,28},{12,0},{16,4},{20,8},{24,12},{28,16},{1,21},{... | collective-permute-start | bytes 36872 | tf_op jit(solution)/shard_map/ppermute | solution.py:73
  64.0 45.3 %collective-permute-start.3 = (bf16[3,2048]{1,0:T(4,128)(2,1)}, bf16[3,2048]{1,0:T(4,128)(2,1)}, u32[]{:S(2)}, u32[]{:S(2)}) collective-permute-start(bf16[3,2048]{1,0:T(4,128)(2,1)} %bitcast.280), channel_id=1, source_target_pairs={{0,16},{4,20},{8,24},{12,28},{16,0},{20,4},{24,8},{28,12},{1,17},{... | collective-permute-start | bytes 36872 | tf_op jit(solution)/shard_map/ppermute | solution.py:73
  74.2 7.1 %copy-start.3 = (f32[8,8,128,128]{3,2,1,0:T(8,128)S(1)}, f32[8,8,128,128]{3,2,1,0:T(8,128)}, u32[]{:S(2)}) copy-start(f32[8,8,128,128]{3,2,1,0:T(8,128)} %param.20) | copy-start | bytes 12582916
  84.6 52.6 %copy-start.5 = (bf16[8,128,128]{2,1,0:T(8,128)(2,1)S(1)}, bf16[8,128,128]{2,1,0:T(8,128)(2,1)}, u32[]{:S(2)}) copy-start(bf16[8,128,128]{2,1,0:T(8,128)(2,1)} %get-tuple-element.32) | copy-start | bytes 786436
  102.0 9.6 %collective-permute-start.4 = (bf16[3,2048]{1,0:T(4,128)(2,1)S(1)}, bf16[3,2048]{1,0:T(4,128)(2,1)S(1)}, u32[]{:S(2)}, u32[]{:S(2)}) collective-permute-start(bf16[3,2048]{1,0:T(4,128)(2,1)S(1)} %bitcast.342), channel_id=1, source_target_pairs={{0,12},{4,16},{8,20},{12,24},{16,28},{20,0},{24,4},{28,8},{1,13},{... | collective-permute-start | bytes 36872 | tf_op jit(solution)/shard_map/ppermute | solution.py:73
  104.3 11.5 %collective-permute-start.6 = (bf16[3,2048]{1,0:T(4,128)(2,1)S(1)}, bf16[3,2048]{1,0:T(4,128)(2,1)S(1)}, u32[]{:S(2)}, u32[]{:S(2)}) collective-permute-start(bf16[3,2048]{1,0:T(4,128)(2,1)S(1)} %bitcast.341), channel_id=1, source_target_pairs={{0,4},{4,8},{8,12},{12,16},{16,20},{20,24},{24,28},{28,0},{1,5},{5... | collective-permute-start | bytes 36872 | tf_op jit(solution)/shard_map/ppermute | solution.py:73
  106.6 58.6 %collective-permute-start.13 = (bf16[8,128,128]{2,1,0:T(8,128)(2,1)S(1)}, bf16[8,128,128]{2,1,0:T(8,128)(2,1)}, u32[]{:S(2)}, u32[]{:S(2)}) collective-permute-start(bf16[8,128,128]{2,1,0:T(8,128)(2,1)S(1)} %get-tuple-element.29), channel_id=1, source_target_pairs={{0,4},{4,8},{8,12},{12,16},{16,20},{20,24},{24,28},{28,0},{1,5},{5... | collective-permute-start | bytes 786440 | tf_op jit(solution)/shard_map/ppermute | solution.py:74
  109.3 54.3 %collective-permute-start.12 = (bf16[8,128,128]{2,1,0:T(8,128)(2,1)}, bf16[8,128,128]{2,1,0:T(8,128)(2,1)}, u32[]{:S(2)}, u32[]{:S(2)}) collective-permute-start(bf16[8,128,128]{2,1,0:T(8,128)(2,1)} %get-tuple-element.30), channel_id=1, source_target_pairs={{0,8},{4,12},{8,16},{12,20},{16,24},{20,28},{24,0},{28,4},{1,9},{5... | collective-permute-start | bytes 786440 | tf_op jit(solution)/shard_map/ppermute | solution.py:74
  111.6 50.2 %collective-permute-start.11 = (bf16[8,128,128]{2,1,0:T(8,128)(2,1)}, bf16[8,128,128]{2,1,0:T(8,128)(2,1)}, u32[]{:S(2)}, u32[]{:S(2)}) collective-permute-start(bf16[8,128,128]{2,1,0:T(8,128)(2,1)} %get-tuple-element.31), channel_id=1, source_target_pairs={{0,12},{4,16},{8,20},{12,24},{16,28},{20,0},{24,4},{28,8},{1,13},{... | collective-permute-start | bytes 786440 | tf_op jit(solution)/shard_map/ppermute | solution.py:74
  112.3 25.0 %collective-permute-start.8 = (bf16[8,128,128]{2,1,0:T(8,128)(2,1)}, bf16[8,128,128]{2,1,0:T(8,128)(2,1)}, u32[]{:S(2)}, u32[]{:S(2)}) collective-permute-start(bf16[8,128,128]{2,1,0:T(8,128)(2,1)} %get-tuple-element.34), channel_id=1, source_target_pairs={{0,24},{4,28},{8,0},{12,4},{16,8},{20,12},{24,16},{28,20},{1,25},{... | collective-permute-start | bytes 786440 | tf_op jit(solution)/shard_map/ppermute | solution.py:74
  115.8 15.6 %collective-permute-start.7 = (bf16[8,128,128]{2,1,0:T(8,128)(2,1)}, bf16[8,128,128]{2,1,0:T(8,128)(2,1)}, u32[]{:S(2)}, u32[]{:S(2)}) collective-permute-start(bf16[8,128,128]{2,1,0:T(8,128)(2,1)} %get-tuple-element.35), channel_id=1, source_target_pairs={{0,28},{4,0},{8,4},{12,8},{16,12},{20,16},{24,20},{28,24},{1,29},{... | collective-permute-start | bytes 786440 | tf_op jit(solution)/shard_map/ppermute | solution.py:74
  131.4 10.9 %collective-permute-start.9 = (bf16[8,128,128]{2,1,0:T(8,128)(2,1)}, bf16[8,128,128]{2,1,0:T(8,128)(2,1)S(1)}, u32[]{:S(2)}, u32[]{:S(2)}) collective-permute-start(bf16[8,128,128]{2,1,0:T(8,128)(2,1)} %get-tuple-element.33), channel_id=1, source_target_pairs={{0,20},{4,24},{8,28},{12,0},{16,4},{20,8},{24,12},{28,16},{1,21},{... | collective-permute-start | bytes 786440 | tf_op jit(solution)/shard_map/ppermute | solution.py:74
  137.3 23.9 %collective-permute-start.10 = (bf16[8,128,128]{2,1,0:T(8,128)(2,1)S(1)}, bf16[8,128,128]{2,1,0:T(8,128)(2,1)S(1)}, u32[]{:S(2)}, u32[]{:S(2)}) collective-permute-start(bf16[8,128,128]{2,1,0:T(8,128)(2,1)S(1)} %copy-done.5), channel_id=1, source_target_pairs={{0,16},{4,20},{8,24},{12,28},{16,0},{20,4},{24,8},{28,12},{1,17},{... | collective-permute-start | bytes 786440 | tf_op jit(solution)/shard_map/ppermute | solution.py:74
  143.0 31.9 %copy-start.13 = (f32[8,1,4,2]{3,2,0,1:T(4,128)S(1)}, f32[8,1,4,2]{3,2,0,1:T(4,128)}, u32[]{:S(2)}) copy-start(f32[8,1,4,2]{3,2,0,1:T(4,128)} %copy.188) | copy-start | bytes 772
  143.0 32.0 %copy-start.14 = (f32[8,1,4,128]{3,2,1,0:T(4,128)S(1)}, f32[8,1,4,128]{3,2,1,0:T(4,128)}, u32[]{:S(2)}) copy-start(f32[8,1,4,128]{3,2,1,0:T(4,128)} %get-tuple-element.47) | copy-start | bytes 49156
  170.7 8.5 %copy-start.2 = (bf16[8,8,128,128]{3,2,1,0:T(8,128)(2,1)S(1)}, bf16[8,8,128,128]{3,2,1,0:T(8,128)(2,1)}, u32[]{:S(2)}) copy-start(bf16[8,8,128,128]{3,2,1,0:T(8,128)(2,1)} %gather_fusion.1) | copy-start | bytes 6291460
  170.7 8.5 %copy-start.7 = (f32[8,1,4,2]{3,2,0,1:T(4,128)S(1)}, f32[8,1,4,2]{3,2,0,1:T(4,128)}, u32[]{:S(2)}) copy-start(f32[8,1,4,2]{3,2,0,1:T(4,128)} %copy.189) | copy-start | bytes 772
  175.0 7.2 %copy-start.12 = (f32[8,1,4,2]{3,2,0,1:T(4,128)S(1)}, f32[8,1,4,2]{3,2,0,1:T(4,128)}, u32[]{:S(2)}) copy-start(f32[8,1,4,2]{3,2,0,1:T(4,128)} %copy.190) | copy-start | bytes 772
  182.1 4.1 %copy-start.8 = (f32[8,1,4,2]{3,2,0,1:T(4,128)S(1)}, f32[8,1,4,2]{3,2,0,1:T(4,128)}, u32[]{:S(2)}) copy-start(f32[8,1,4,2]{3,2,0,1:T(4,128)} %copy.191) | copy-start | bytes 772
  186.2 3.8 %copy-start.11 = (f32[8,1,4,2]{3,2,0,1:T(4,128)S(1)}, f32[8,1,4,2]{3,2,0,1:T(4,128)}, u32[]{:S(2)}) copy-start(f32[8,1,4,2]{3,2,0,1:T(4,128)} %copy.192) | copy-start | bytes 772
  190.2 4.2 %copy-start.9 = (f32[8,1,4,2]{3,2,0,1:T(4,128)S(1)}, f32[8,1,4,2]{3,2,0,1:T(4,128)}, u32[]{:S(2)}) copy-start(f32[8,1,4,2]{3,2,0,1:T(4,128)} %copy.193) | copy-start | bytes 772
  194.4 4.4 %copy-start.10 = (f32[8,1,4,2]{3,2,0,1:T(4,128)S(1)}, f32[8,1,4,2]{3,2,0,1:T(4,128)}, u32[]{:S(2)}) copy-start(f32[8,1,4,2]{3,2,0,1:T(4,128)} %copy.194) | copy-start | bytes 772
  202.6 2.0 copy-start.1
  202.6 4.7 %copy-start.17 = (f32[128]{0:T(128)S(1)}, f32[128]{0:T(128)}, u32[]{:S(2)}) copy-start(f32[128]{0:T(128)} %param.30) | copy-start | bytes 1540
  204.6 6.5 %copy-start.6 = (s32[32,10]{0,1:T(8,128)S(1)}, s32[32,10]{0,1:T(8,128)}, u32[]{:S(2)}) copy-start(s32[32,10]{0,1:T(8,128)} %param.33) | copy-start | bytes 3844
  204.6 35.9 %copy-start.4 = (bf16[32,2048]{1,0:T(8,128)(2,1)S(1)}, bf16[32,2048]{1,0:T(8,128)(2,1)}, u32[]{:S(2)}) copy-start(bf16[32,2048]{1,0:T(8,128)(2,1)} %param.19) | copy-start | bytes 393220
  206.7 34.9 %copy-start.15 = (f32[2048]{0:T(1024)S(1)}, f32[2048]{0:T(1024)}, u32[]{:S(2)}) copy-start(f32[2048]{0:T(1024)} %param.32) | copy-start | bytes 24580
  260.7 8.0 %copy-start.16 = (f32[32,10]{0,1:T(8,128)S(1)}, f32[32,10]{0,1:T(8,128)}, u32[]{:S(2)}) copy-start(f32[32,10]{0,1:T(8,128)} %param.34) | copy-start | bytes 3844
  264.9 17.7 %all-to-all-start.1 = ((bf16[1,8,16,2048]{3,2,0,1:T(8,128)(2,1)}), bf16[1,8,16,2048]{3,2,0,1:T(8,128)(2,1)S(1)}, u32[]{:S(2)}, u32[]{:S(2)}) async-start(bf16[1,8,16,2048]{3,2,0,1:T(8,128)(2,1)} %bitcast.297), calls=%async_computation.1 | async-start | bytes 1048576 | tf_op jit(solution)/shard_map/all_to_all | solution.py:171
  268.6 33.2 %reduce-scatter.2.cloned.1.call-start = ((), (), s32[]{:S(2)}) async-start(), calls=%async_computation.4 | async-start | bytes 163840 | tf_op jit(solution)/shard_map/reduce_scatter | solution.py:175
Sparse Core Ops, SparseCore 0:
  211.2 29.2 all-reduce.1
  283.7 18.0 reduce-scatter.1

commit v2 on v0

v2 whole, which is shorter than its diff:
```python
import functools
import jax
import jax.numpy as jnp
from jax import lax
from jax.experimental import pallas as pl
from jax.experimental.pallas import tpu as pltpu
from jax.sharding import PartitionSpec as P

epsilon = 1e-06
MESH = pl.DeviceIdType.MESH
bf16, f32 = jnp.bfloat16, jnp.float32


def silu(x):
    return x * (1.0 / (1.0 + jnp.exp(-x)))


def kernel(
    G, E, offsets, S,
    slot_ref, tok_ref, own_ref, wts_ref, tails_ref, gain_ref, wba_ref, conv_ref, alog_ref, dtb_ref,
    ngain_ref, pgain_ref, sel_ref, wq_hbm, wo_hbm, gu_hbm, dn_hbm, st_hbm,
    lay_ref, ct_ref, st_out,
    wq, wo, gu, dn, st, st_send, st_recv, st_new, tok_recv, wts_all, x_ref, nrm, gated,
    ck_send, ck_recv, hp_send, hp_recv, res, moe, hidden, hid, y_send, y_recv, base, part, z_recv,
    load_sem, out_sem, tok_ss, tok_rs, st_ss, st_rs, ck_ss, ck_rs, w_ss, w_rs,
    hp_ss, hp_rs, g_ss, g_rs, e_ss, e_rs, y_ss, y_rs, z_ss, z_rs,
):
    R = len(offsets)
    ROWS = S * R
    HP = conv_ref.shape[1] // 512
    HV = 2 * HP
    L = gu.shape[0]
    D = x_ref.shape[1]
    F = dn.shape[1]
    share = D // E
    g = lax.axis_index("group")
    e = lax.axis_index("ep")

    loads = [
        pltpu.make_async_copy(src, dst, load_sem.at[n])
        for n, (src, dst) in enumerate(
            [(st_hbm, st), (wq_hbm, wq), (wo_hbm, wo), (gu_hbm, gu), (dn_hbm, dn)]
        )
    ]
    for copy in loads:
        copy.start()

    barrier = pltpu.get_barrier_semaphore()

    def greet_group(k, carry):
        pl.semaphore_signal(barrier, inc=1, device_id=(lax.rem(g + k, G), e), device_id_type=MESH)
        return carry

    def greet_ep(m, carry):
        pl.semaphore_signal(barrier, inc=1, device_id=(g, lax.rem(e + m, E)), device_id_type=MESH)
        return carry

    lax.fori_loop(1, G, greet_group, 0)
    lax.fori_loop(1, E, greet_ep, 0)
    pl.semaphore_wait(barrier, G - 1 + E - 1)

    def move(src, dst, ss, rs, i, group):
        if offsets[i] % G == 0:
            return pltpu.make_async_copy(src, dst, rs.at[i]), False
        return (
            pltpu.make_async_remote_copy(
                src_ref=src, dst_ref=dst, send_sem=ss.at[i], recv_sem=rs.at[i],
                device_id=(group, e), device_id_type=MESH,
            ),
            True,
        )

    def finish(copies):
        for copy, _ in copies:
            copy.wait()

    tok_copies = []
    for i in range(R):
        rows = pl.ds(16 * i, 16)
        pair = move(tok_ref.at[rows], tok_recv.at[rows], tok_ss, tok_rs, i, lax.rem(g + offsets[i], G))
        pair[0].start()
        tok_copies.append(pair)

    def wts_copy(k):
        to = lax.rem(g + k, G)
        return pltpu.make_async_remote_copy(
            src_ref=wts_ref.at[to], dst_ref=wts_all.at[k], send_sem=w_ss.at[k], recv_sem=w_rs.at[k],
            device_id=(to, e), device_id_type=MESH,
        )

    lax.fori_loop(1, G, lambda k, c: (wts_copy(k).start(), c)[1], 0)
    wts_all[0] = wts_ref[g]

    loads[0].wait()
    st_copies = []
    for i in range(R):
        st_send[i] = st[slot_ref[i]].astype(bf16)
        pair = move(st_send.at[i], st_recv.at[i], st_ss, st_rs, i, lax.rem(g + G - offsets[i], G))
        pair[0].start()
        st_copies.append(pair)

    finish(tok_copies)
    parts = sel_ref.shape[0]
    width = D // parts
    for q in range(parts):
        x_ref[:, q * width : (q + 1) * width] = jnp.dot(
            sel_ref[q], tok_recv[...], preferred_element_type=f32
        )

    def normalize(x, gain):
        return x * lax.rsqrt(jnp.mean(x * x, axis=-1, keepdims=True) + epsilon) * gain

    nrm[:ROWS] = normalize(x_ref[...], gain_ref[...]).astype(bf16)
    nrm[ROWS:] = normalize(own_ref[...].astype(f32), gain_ref[...]).astype(bf16)

    rates = jnp.dot(nrm[:ROWS], wba_ref[...], preferred_element_type=f32)
    write_rate = 1.0 / (1.0 + jnp.exp(-rates))
    shifted = rates + dtb_ref[...]
    softplus = jnp.maximum(shifted, 0.0) + jnp.log1p(jnp.exp(-jnp.abs(shifted)))
    decays = jnp.exp(-jnp.exp(alog_ref[...]) * softplus)
    request_of = lax.broadcasted_iota(jnp.int32, (2 * ROWS, 128), 0) % R

    loads[1].wait()
    for h in range(HP):
        projected = jnp.dot(nrm[...], wq[:, h * 768 : (h + 1) * 768], preferred_element_type=f32)
        rounded = projected[:, :512].astype(bf16)
        ct_ref[:, h * 512 : (h + 1) * 512] = rounded[ROWS:]
        entered = rounded[:ROWS].astype(f32)
        window = [tails_ref[n][:, h * 512 : (h + 1) * 512] for n in range(3)]
        window += [entered[s * R : (s + 1) * R] for s in range(S)]
        taps = [conv_ref[n : n + 1, h * 512 : (h + 1) * 512] for n in range(4)]
        ks, qs, vs = [], [], []
        for s in range(S):
            mixed = taps[0] * window[s]
            for n in range(1, 4):
                mixed = mixed + taps[n] * window[s + n]
            out = silu(mixed)
            q_, k_ = out[:, :128], out[:, 128:256]
            qs.append(q_ * lax.rsqrt(jnp.sum(q_ * q_, axis=-1, keepdims=True) + epsilon) * 128 ** (-0.5))
            ks.append(k_ * lax.rsqrt(jnp.sum(k_ * k_, axis=-1, keepdims=True) + epsilon))
            vs.append(out[:, 256:])
        both = jnp.concatenate(ks + qs, axis=0).astype(bf16)
        kk = {(t, s): jnp.sum(ks[t] * ks[s], axis=-1, keepdims=True) for s in range(S) for t in range(s)}
        kq = {(t, s): jnp.sum(ks[t] * qs[s], axis=-1, keepdims=True) for s in range(S) for t in range(s + 1)}
        for s in range(S):
            for i in range(R):
                row = S * HV + h * S + s
                ck_send[i, row : row + 1, :] = ks[s][i : i + 1]
        for p in range(2):
            hv = 2 * h + p

            def apply(i, acc):
                product = jnp.dot(both, st_send[i, hv], preferred_element_type=f32)
                return jnp.where(request_of == i, product, acc)

            start = lax.fori_loop(0, R, apply, jnp.zeros((2 * ROWS, 128), f32))
            dec = [decays[s * R : (s + 1) * R, 4 * h + 2 + p : 4 * h + 3 + p] for s in range(S)]
            beta = [write_rate[s * R : (s + 1) * R, 4 * h + p : 4 * h + p + 1] for s in range(S)]
            kept = []
            total = None
            for s in range(S):
                total = dec[s] if total is None else total * dec[s]
                kept = [c * dec[s] for c in kept]
                guess = total * start[s * R : (s + 1) * R]
                for t in range(s):
                    guess = guess + kk[t, s] * kept[t]
                kept.append(beta[s] * (vs[s][:, p * 128 : (p + 1) * 128] - guess))
                read = total * start[ROWS + s * R : ROWS + (s + 1) * R]
                for t in range(s + 1):
                    read = read + kq[t, s] * kept[t]
                z = projected[s * R : (s + 1) * R, 512 + p * 128 : 640 + p * 128]
                gated[s * R : (s + 1) * R, hv * 128 : (hv + 1) * 128] = (
                    normalize(read, ngain_ref[...]) * silu(z)
                )
            spread = jnp.broadcast_to(total, (R, 128))
            for i in range(R):
                for s in range(S):
                    ck_send[i, hv * S + s : hv * S + s + 1, :] = kept[s][i : i + 1]
                row = S * HV + S * HP + hv
                ck_send[i, row : row + 1, :] = spread[i : i + 1]
    used = S * HV + S * HP + HV
    if used < ck_send.shape[1]:
        for i in range(R):
            ck_send[i, used:, :] = jnp.zeros((ck_send.shape[1] - used, 128), f32)

    loads[2].wait()
    gated16 = gated[...].astype(bf16)
    for q in range(E):
        out = jnp.dot(gated16, wo[:, q * share : (q + 1) * share], preferred_element_type=f32)
        res[q] = x_ref[:, q * share : (q + 1) * share] + out
        hp_send[q] = out.astype(bf16)

    def hp_copy(m):
        return pltpu.make_async_remote_copy(
            src_ref=hp_send, dst_ref=hp_recv.at[m - 1], send_sem=hp_ss.at[m - 1],
            recv_sem=hp_rs.at[m - 1], device_id=(g, lax.rem(e + m, E)), device_id_type=MESH,
        )

    for m in range(1, E):
        hp_copy(m).start()
    ck_copies = []
    for i in range(R):
        pair = move(ck_send.at[i], ck_recv.at[i], ck_ss, ck_rs, i, lax.rem(g + G - offsets[i], G))
        pair[0].start()
        ck_copies.append(pair)
    for m in range(1, E):
        hp_copy(m).wait()
    square = jnp.zeros((ROWS, 1), f32)
    for q in range(E):
        value = res[q]
        for m in range(1, E):
            value = value + hp_recv[m - 1, q].astype(f32)
        res[q] = value
        square = square + jnp.sum(value * value, axis=-1, keepdims=True)
    scale = lax.rsqrt(square / D + epsilon)

    def rows_of(block):
        return pl.ds(pl.multiple_of(block * ROWS, ROWS), ROWS)

    moe[e, rows_of(g)] = (res[e] * scale * pgain_ref[e]).astype(bf16)

    def group_copy(k):
        place = moe.at[e, rows_of(g)]
        return pltpu.make_async_remote_copy(
            src_ref=place, dst_ref=place, send_sem=g_ss.at[k], recv_sem=g_rs.at[k],
            device_id=(lax.rem(g + k, G), e), device_id_type=MESH,
        )

    def arrived(k):
        place = moe.at[e, rows_of(lax.rem(g + G - k, G))]
        return pltpu.make_async_remote_copy(
            src_ref=place, dst_ref=place, send_sem=g_ss.at[k], recv_sem=g_rs.at[k],
            device_id=(lax.rem(g + k, G), e), device_id_type=MESH,
        )

    def pass_on(k, m):
        place = moe.at[e, rows_of(lax.rem(g + G - k, G))]
        return pltpu.make_async_remote_copy(
            src_ref=place, dst_ref=place, send_sem=e_ss.at[m - 1, k], recv_sem=e_rs.at[m - 1, k],
            device_id=(g, lax.rem(e + m, E)), device_id_type=MESH,
        )

    def taken(k, m):
        place = moe.at[lax.rem(e + E - m, E), rows_of(lax.rem(g + G - k, G))]
        return pltpu.make_async_remote_copy(
            src_ref=place, dst_ref=place, send_sem=e_ss.at[m - 1, k], recv_sem=e_rs.at[m - 1, k],
            device_id=(g, lax.rem(e + m, E)), device_id_type=MESH,
        )

    lax.fori_loop(1, G, lambda k, c: (group_copy(k).start(), c)[1], 0)
    for m in range(1, E):
        pass_on(0, m).start()

    base[...] = jnp.zeros_like(base)
    row_request = lax.broadcasted_iota(jnp.int32, (ROWS, share), 0) % R
    for i in range(R):
        base[lax.rem(g + G - offsets[i], G)] += jnp.where(row_request == i, res[e], 0.0)

    def forward(k, carry):
        arrived(k).wait_recv()
        for m in range(1, E):
            pass_on(k, m).start()
        return carry

    lax.fori_loop(1, G, forward, 0)

    def collect(k, carry):
        for m in range(1, E):
            taken(k, m).wait_recv()
        return carry

    lax.fori_loop(0, G, collect, 0)
    loads[3].wait()
    loads[4].wait()
    for l in range(L):
        halves = jnp.dot(moe[0], gu[l, :share], preferred_element_type=f32)
        for q in range(1, E):
            halves = halves + jnp.dot(
                moe[q], gu[l, q * share : (q + 1) * share], preferred_element_type=f32
            )
        hidden[l] = silu(halves[:, :F]) * halves[:, F:]
    row_hidden = lax.broadcasted_iota(jnp.int32, (ROWS, F), 0) % R

    def regroup(d, carry):
        for l in range(L):
            total = jnp.zeros((ROWS, F), f32)
            for i in range(R):
                total = jnp.where(
                    row_hidden == i, hidden[l, rows_of(lax.rem(d + offsets[i], G))], total
                )
            hid[l, rows_of(d)] = total.astype(bf16)
        return carry

    lax.fori_loop(0, G, regroup, 0)

    lax.fori_loop(1, G, lambda k, c: (wts_copy(k).wait(), c)[1], 0)
    picked = lax.broadcasted_iota(jnp.int32, (ROWS, 128), 0) == lax.broadcasted_iota(
        jnp.int32, (ROWS, 128), 1
    )
    for q in range(E):
        for l in range(L):
            out = jnp.dot(hid[l], dn[l, :, q * share : (q + 1) * share], preferred_element_type=f32)
            hidden_rows = out.astype(bf16).astype(f32)
            if l == 0:
                sums = [0.0] * G
            for d in range(G):
                tile = wts_all[lax.rem(g + G - d, G)]
                weight = jnp.sum(jnp.where(picked, tile[l : l + 1], 0.0), axis=-1, keepdims=True)
                sums[d] = sums[d] + weight * hidden_rows[d * ROWS : (d + 1) * ROWS]
        for d in range(G):
            y_send[q, d * ROWS : (d + 1) * ROWS] = sums[d].astype(bf16)

    def y_copy(k, m):
        d = lax.rem(g + k, G)
        to = lax.rem(e + m, E)
        return pltpu.make_async_remote_copy(
            src_ref=y_send.at[to, rows_of(d)], dst_ref=y_recv.at[m - 1, rows_of(d)],
            send_sem=y_ss.at[m - 1, k], recv_sem=y_rs.at[m - 1, k],
            device_id=(g, to), device_id_type=MESH,
        )

    def z_copy(k):
        to = lax.rem(g + k, G)
        return pltpu.make_async_remote_copy(
            src_ref=part.at[to], dst_ref=z_recv.at[k], send_sem=z_ss.at[k], recv_sem=z_rs.at[k],
            device_id=(to, e), device_id_type=MESH,
        )

    def y_start(k, carry):
        for m in range(1, E):
            y_copy(lax.rem(k, G), m).start()
        return carry

    lax.fori_loop(1, G + 1, y_start, 0)

    def y_total(k):
        d = lax.rem(g + k, G)
        total = base[d] + y_send[e, rows_of(d)].astype(f32)
        for m in range(1, E):
            y_copy(k, m).wait_recv()
            total = total + y_recv[m - 1, rows_of(d)].astype(f32)
        return total

    def combine(k, carry):
        part[lax.rem(g + k, G)] = y_total(k).astype(bf16)
        z_copy(k).start()
        return carry

    lax.fori_loop(1, G, combine, 0)
    final = y_total(0)

    finish(ck_copies)
    finish(st_copies)

    def put(i):
        return pltpu.make_async_copy(st_new.at[i], st_out.at[i], out_sem.at[i])

    def renew(i, carry):
        for hv in range(HV):
            h = hv // 2
            k4 = ck_recv[i, S * HV + h * S : S * HV + (h + 1) * S]
            c4 = ck_recv[i, hv * S : (hv + 1) * S]
            row = S * HV + S * HP + hv
            change = lax.dot_general(k4, c4, (((0,), (0,)), ((), ())), preferred_element_type=f32)
            st_new[i, hv] = ck_recv[i, row : row + 1] * st_recv[i, hv].astype(f32) + change
        put(i).start()
        return carry

    lax.fori_loop(0, R, renew, 0)
    for k in range(1, G):
        z_copy(k).wait_recv()
        final = final + z_recv[k].astype(f32)
    lay_ref[...] = final.astype(bf16)

    def drain(k, carry):
        group_copy(k).wait_send()
        z_copy(k).wait_send()
        return carry

    lax.fori_loop(1, G, drain, 0)

    def drain_ep(k, carry):
        for m in range(1, E):
            pass_on(k, m).wait_send()
            y_copy(k, m).wait_send()
        return carry

    lax.fori_loop(0, G, drain_ep, 0)
    lax.fori_loop(0, R, lambda i, c: (put(i).wait(), c)[1], 0)


def body(
    tokens, prefill_states, prefill_tails, src_group, src_slot, in_gain, w_qkvz, w_ba, conv_weight,
    a_log, dt_bias, norm_gain, w_out, post_gain, expert_ids, gate_probs, gate_up_weight, down_weight,
):
    G = lax.axis_size("group")
    E = lax.axis_size("ep")
    g = lax.axis_index("group")
    e = lax.axis_index("ep")
    R, HV = prefill_states.shape[:2]
    ROWS, D = tokens.shape
    S = ROWS // R
    HP = HV // 2
    L = gate_up_weight.shape[0]
    F = down_weight.shape[1]
    C = conv_weight.shape[1]
    share = D // E
    stride = G // R
    offsets = [
        which * stride if stride == 1 or which == R // 2 else (which * stride - 1) % G
        for which in range(R)
    ]
    offset_array = jnp.array(offsets, jnp.int32)
    slot_offsets = (src_group[0] % G).astype(jnp.int32)
    matches = (slot_offsets[:, None] == offset_array[None, :]).astype(jnp.int32)
    request_at = jnp.argmax(matches, axis=0)
    place_of = jnp.argmax(matches, axis=1)
    slots = src_slot[(g - offset_array) % G, request_at].astype(jnp.int32)

    parts = 16 // S
    ordered = tokens.reshape(R, S, D)[request_at]
    tok = ordered.reshape(R * 16, D // parts)
    rows = jnp.arange(ROWS)
    source = (rows % R) * 16 + (rows // R) * parts
    sel = (
        (source[None, :, None] + jnp.arange(parts)[:, None, None]) == jnp.arange(R * 16)[None, None, :]
    ).astype(bf16)

    expert_of = (jnp.arange(G)[:, None] * E + e) * L + jnp.arange(L)[None, :]
    hits = expert_ids[None, None] == expert_of[:, :, None, None]
    dense = jnp.sum(jnp.where(hits, gate_probs[None, None], 0.0), axis=-1)
    dense = dense.reshape(G, L, R, S)[:, :, request_at].transpose(0, 1, 3, 2).reshape(G, L, ROWS)
    wts = jnp.pad(dense, ((0, 0), (0, 8 - L), (0, 128 - ROWS)))

    tails = prefill_tails[slots].transpose(1, 0, 2).astype(f32)
    zero = jnp.zeros((HP, 2), f32)
    alog = jnp.concatenate([zero, a_log.reshape(HP, 2)], axis=1).reshape(1, 4 * HP)
    dtb = jnp.concatenate([zero, dt_bias.reshape(HP, 2)], axis=1).reshape(1, 4 * HP)

    ck_rows = -(-(S * HV + S * HP + HV) // 8) * 8
    vm = pl.BlockSpec(memory_space=pltpu.VMEM)
    anywhere = pl.BlockSpec(memory_space=pl.ANY)
    dma = pltpu.SemaphoreType.DMA
    V = pltpu.VMEM
    layer, conv_rows, states = pl.pallas_call(
        functools.partial(kernel, G, E, tuple(offsets), S),
        out_shape=(
            jax.ShapeDtypeStruct((ROWS, share), bf16),
            jax.ShapeDtypeStruct((ROWS, C), bf16),
            jax.ShapeDtypeStruct(prefill_states.shape, f32),
        ),
        in_specs=[pl.BlockSpec(memory_space=pltpu.SMEM)] + [vm] * 12 + [anywhere] * 5,
        out_specs=(vm, vm, anywhere),
        scratch_shapes=[
            V(w_qkvz.shape, bf16), V(w_out.shape, bf16), V(gate_up_weight.shape, bf16),
            V(down_weight.shape, bf16), V(prefill_states.shape, f32),
            V(prefill_states.shape, bf16), V(prefill_states.shape, bf16), V(prefill_states.shape, f32),
            V(tok.shape, bf16), V((G, 8, 128), f32), V((ROWS, D), f32), V((2 * ROWS, D), bf16),
            V((ROWS, HV * 128), f32), V((R, ck_rows, 128), f32), V((R, ck_rows, 128), f32),
            V((E, ROWS, share), bf16), V((E - 1, E, ROWS, share), bf16), V((E, ROWS, share), f32),
            V((E, G * ROWS, share), bf16), V((L, G * ROWS, F), f32), V((L, G * ROWS, F), bf16),
            V((E, G * ROWS, share), bf16), V((E - 1, G * ROWS, share), bf16),
            V((G, ROWS, share), f32), V((G, ROWS, share), bf16), V((G, ROWS, share), bf16),
            dma((5,)), dma((R,)), dma((R,)), dma((R,)), dma((R,)), dma((R,)), dma((R,)), dma((R,)),
            dma((G,)), dma((G,)), dma((E - 1,)), dma((E - 1,)), dma((G,)), dma((G,)),
            dma((E - 1, G)), dma((E - 1, G)), dma((E - 1, G)), dma((E - 1, G)), dma((G,)), dma((G,)),
        ],
        compiler_params=pltpu.CompilerParams(
            collective_id=0, has_side_effects=True, vmem_limit_bytes=58 * 2**20
        ),
    )(
        slots, tok, tokens, wts, tails, in_gain.reshape(1, D), w_ba, conv_weight, alog, dtb,
        norm_gain.reshape(1, 128), post_gain.reshape(E, 1, share), sel,
        w_qkvz, w_out, gate_up_weight, down_weight, prefill_states,
    )
    layer_out = layer.reshape(S, R, share)[:, place_of].transpose(1, 0, 2).reshape(ROWS, share)
    new_tails = conv_rows.reshape(R, S, C)[:, S - 3 :]
    return (layer_out, states[place_of], new_tails)


def solution(mesh):
    in_specs = (
        P("group", None), P("group", "ep", None, None), P("group", None, "ep"), P(), P(), P(),
        P(None, "ep"), P(None, "ep"), P(None, "ep"), P("ep"), P("ep"), P(), P("ep", None), P(),
        P("group", None), P("group", None), P(("group", "ep"), None, None),
        P(("group", "ep"), None, None),
    )
    out_specs = (P("group", "ep"), P("group", "ep", None, None), P("group", None, "ep"))
    return jax.shard_map(body, mesh=mesh, in_specs=in_specs, out_specs=out_specs, check_vma=False)
```

time: 811 us -> 119 us (0.15)
  waiting for transfers between devices: 618 us -> 0 us
  blocking collectives: 105 us -> 0 us
  Pallas kernels: 0 us -> 95.3 us
  matrix products: 45.2 us -> 0 us
  between operations: 14.2 us -> 0.73 us
    all_gather x1 -> x0, waiting for transfers between devices: 554 us -> none  [body(): lax.all_gather(prefill_states, 'group', axis=0, tiled=True)]
    pallas_call x0 -> x1, Pallas kernels: none -> 95.3 us  [body(): pl.pallas_call(functools.partial(kernel, G, E, tuple(offsets), S), out_sh...]
    all_gather x1 -> x0, blocking collectives: 86 us -> none  [body(): lax.all_gather(prefill_tails.astype(jnp.float32), 'group', axis=0, tiled=...]
    dot_general x15 -> x0, matrix products: 45.2 us -> none  [the longest x4 15.8 us: body(): jnp.einsum('rqk,rqhkv->rqhv', keys[:, token_step], memory, precision=high...]
    psum x1 -> x0, waiting for transfers between devices: 31.9 us -> none  [body(): residual = input_rows + lax.psum(head_part, 'ep')]
    all_to_all x1 -> x0, blocking collectives: 18.7 us -> none  [body(): lax.all_to_all(send_rows, 'group', split_axis=1, concat_axis=1, tiled=True)]
    reduce_scatter x1 -> x0, waiting for transfers between devices: 17.4 us -> none  [body(): lax.psum_scatter(weighted.astype(jnp.bfloat16), 'ep', scatter_dimension=1...]
    all_to_all x1 -> x0, waiting for transfers between devices: 13.8 us -> none  [body(): lax.all_to_all(expert_rows, 'group', split_axis=1, concat_axis=1, tiled=T...]
  transfers between devices with their start and end apart: 4 -> 0, of which waited for: 4 -> 0; matrix products, arithmetic and copies ran while one was open for 2% -> 0% of each run, Pallas kernels for 0% -> 0%
where the time goes in v2:
time: 119 us
  Pallas kernels  95.3 us (80%)
  local copies, waits for them, and re-layouts  18.5 us (16%)
  other arithmetic  4.26 us (4%)
    pallas_call x1, Pallas kernels, body(): pl.pallas_call(functools.partial(kernel, G, E, tuple(offsets), S), out_sh...  95.3 us
    gather x1, local copies, waits for them, and re-layouts, body(): return (layer_out, states[place_of], new_tails)  5.05 us
    unnamed x8, local copies, waits for them, and re-layouts  2.58 us

profile of v2, /device:TPU:0, one launch (start us, length us, event | category | flops | bytes accessed | tf_op | source)
XLA Modules:
  0.0 118.8 jit_solution(15443377246990585035)
XLA Ops:
  0.6 0.0 copy-start
  0.7 0.7 and_select_fusion.2
  1.4 0.7 convert_reduce_fusion
  2.1 0.6 convert_reduce_fusion.1
  2.7 1.3 %gather_fusion = s32[8]{0:T(128)S(1)} fusion(s32[8,8]{1,0:T(8,128)} %param.23, s32[8]{0:T(128)S(1)} %get-tuple-element.14), kind=kCustom, calls=%fused_computation | custom fusion | bytes 128 | tf_op jit(solution)/shard_map/gather | solution.py:418
  4.0 0.0 copy-start.2
  4.1 0.7 reshape.160
  4.8 0.1 concatenate.10
  4.9 0.6 reshape.161.alog_ref
  5.5 0.7 reshape.162
  6.2 0.1 concatenate.11
  6.3 0.6 reshape.163.dtb_ref
  6.9 0.8 select_reduce_fusion
  7.7 0.1 copy.33
  7.8 0.6 gather_fusion.2
  8.3 0.1 copy.34
  8.4 0.1 reshape.158
  8.5 0.6 pad.6.wts_ref
  9.1 0.7 fusion.sel_ref
  9.8 0.0 copy-done
  9.8 0.8 gather_fusion.3
  10.7 0.7 convert_bitcast_fusion.tails_ref
  11.4 1.0 reshape.155
  12.3 0.7 gather_fusion.1
  13.0 0.7 reshape.156.tok_ref
  13.7 1.8 %copy.35.wba_ref = bf16[2048,16]{1,0:T(8,128)(2,1)} copy(bf16[2048,16]{0,1:T(8,128)(2,1)} %param.26) | data formatting | bytes 131072 | tf_op args[7]
  15.6 0.0 copy-done.2
  15.6 95.3 %shard_map.202 = (bf16[32,512]{1,0:T(8,128)(2,1)}, bf16[32,2048]{1,0:T(8,128)(2,1)}, f32[8,8,128,128]{3,2,1,0:T(8,128)}) custom-call(s32[8]{0:T(128)} %copy-done.2, bf16[128,512]{1,0:T(8,128)(2,1)} %reshape.156.tok_ref, bf16[32,2048]{1,0:T(8,128)(2,1)} %own_ref.1, f32[8,8,128]{2,1,0:T(8,128)} %pad.6.wts_ref, f32[3,8,2048]{2,1,0:T(8,128)} %convert_bitcast_fusion.tails_ref, ...), custom_call_target="tpu_custom_call" | custom-call | tf_op jit(solution)/shard_map/pallas_call | solution.py:445
  110.9 0.8 copy.36
  111.7 0.6 gather_fusion.4
  112.3 0.0 copy-start.1
  112.3 5.1 %gather_fusion.5 = f32[8,8,128,128]{3,2,1,0:T(8,128)} fusion(f32[8,8,128,128]{3,2,1,0:T(8,128)} %get-tuple-element.11, s32[1024]{0:T(1024)S(1)} %pad_clamp_fusion), kind=kCustom, calls=%fused_computation.5 | custom fusion | bytes 8388640 | tf_op jit(solution)/shard_map/gather | solution.py:478
  117.4 0.6 reshape.167
  118.0 0.0 copy-done.1
  118.0 0.1 reshape.168
  118.0 0.1 slice.20
  118.1 0.7 copy.38
  (9 shorter events, 0.1 us)
Async XLA Ops:
  0.6 9.2 %copy-start = (bf16[8,3,2048]{2,0,1:T(8,128)(2,1)S(1)}, bf16[8,3,2048]{2,0,1:T(8,128)(2,1)}, u32[]{:S(2)}) copy-start(bf16[8,3,2048]{2,0,1:T(8,128)(2,1)} %param.21) | copy-start | bytes 294916
  4.0 11.5 %copy-start.2 = (s32[8]{0:T(128)}, s32[8]{0:T(128)S(1)}, u32[]{:S(2)}) copy-start(s32[8]{0:T(128)S(1)} %gather_fusion) | copy-start | bytes 100
  112.3 5.7 %copy-start.1 = (bf16[32,2048]{1,0:T(8,128)(2,1)S(1)}, bf16[32,2048]{1,0:T(8,128)(2,1)}, u32[]{:S(2)}) copy-start(bf16[32,2048]{1,0:T(8,128)(2,1)} %get-tuple-element.12) | copy-start | bytes 393220

commit v3 on v2

--- a/solution.py
+++ b/solution.py
@@ -17,12 +17,12 @@
 
 def kernel(
     G, E, offsets, S,
-    slot_ref, tok_ref, own_ref, wts_ref, tails_ref, gain_ref, wba_ref, conv_ref, alog_ref, dtb_ref,
-    ngain_ref, pgain_ref, sel_ref, wq_hbm, wo_hbm, gu_hbm, dn_hbm, st_hbm,
-    lay_ref, ct_ref, st_out,
-    wq, wo, gu, dn, st, st_send, st_recv, st_new, tok_recv, wts_all, x_ref, nrm, gated,
-    ck_send, ck_recv, hp_send, hp_recv, res, moe, hidden, hid, y_send, y_recv, base, part, z_recv,
-    load_sem, out_sem, tok_ss, tok_rs, st_ss, st_rs, ck_ss, ck_rs, w_ss, w_rs,
+    sgroup_ref, sslot_ref, alog_ref, dtb_ref, own_ref, ids_ref, probs_ref, tail_ref, gain_ref, wba_ref,
+    conv_ref, ngain_ref, pgain_ref, wq_hbm, wo_hbm, gu_hbm, dn_hbm, st_hbm,
+    lay_ref, ct_ref, st_recv, ck_recv,
+    wq, wo, gu, dn, st, st_send, own32, tok_ref, tails_ref, wts_ref, tok_recv, wts_all, x_ref, nrm,
+    gated, ck_send, hp_send, hp_recv, res, pgain, moe, hidden, hid, y_send, y_recv, base, part, z_recv,
+    load_sem, tok_ss, tok_rs, st_ss, st_rs, ck_ss, ck_rs, w_ss, w_rs,
     hp_ss, hp_rs, g_ss, g_rs, e_ss, e_rs, y_ss, y_rs, z_ss, z_rs,
 ):
     R = len(offsets)
@@ -45,6 +45,39 @@
     for copy in loads:
         copy.start()
 
+    asked = [sgroup_ref[0, j] for j in range(R)]
+    request_at = []
+    for offset in offsets:
+        found = jnp.int32(0)
+        for j in range(R):
+            found = jnp.where(asked[j] == offset, j, found)
+        request_at.append(found)
+    slots = [sslot_ref[lax.rem(g + G - offsets[i], G), request_at[i]] for i in range(R)]
+    quarter = 16 // S
+    width = D // quarter
+    own = own_ref[...].astype(f32)
+    for j in range(R):
+        own32[j, :S, :] = own[j * S : (j + 1) * S]
+    for i in range(R):
+        four = own32[request_at[i], :S, :]
+        tok_ref[16 * i : 16 * (i + 1), :] = jnp.concatenate(
+            [four[:, q * width : (q + 1) * width] for q in range(quarter)], axis=0
+        ).astype(bf16)
+        tail = tail_ref[slots[i]].astype(f32)
+        for n in range(3):
+            tails_ref[n, i : i + 1, :] = tail[n : n + 1]
+    diagonal = lax.broadcasted_iota(jnp.int32, (ROWS, 128), 0) == lax.broadcasted_iota(
+        jnp.int32, (ROWS, 128), 1
+    )
+    wts_ref[...] = jnp.zeros_like(wts_ref)
+    for to in range(G):
+        for l in range(L):
+            named = ids_ref[...] == (to * E + e) * L + l
+            weight = jnp.sum(jnp.where(named, probs_ref[...], 0.0), axis=-1, keepdims=True)
+            wts_ref[to, l : l + 1, :] = jnp.sum(
+                jnp.where(diagonal, weight, 0.0), axis=0, keepdims=True
+            )
+
     barrier = pltpu.get_barrier_semaphore()
 
     def greet_group(k, carry):
@@ -94,17 +127,18 @@
     loads[0].wait()
     st_copies = []
     for i in range(R):
-        st_send[i] = st[slot_ref[i]].astype(bf16)
+        st_send[i] = st[slots[i]].astype(bf16)
         pair = move(st_send.at[i], st_recv.at[i], st_ss, st_rs, i, lax.rem(g + G - offsets[i], G))
         pair[0].start()
         st_copies.append(pair)
 
     finish(tok_copies)
-    parts = sel_ref.shape[0]
-    width = D // parts
-    for q in range(parts):
+    to_row = lax.broadcasted_iota(jnp.int32, (ROWS, 16 * R), 0)
+    from_row = lax.broadcasted_iota(jnp.int32, (ROWS, 16 * R), 1)
+    for q in range(quarter):
+        select = from_row == (to_row % R) * 16 + q * S + to_row // R
         x_ref[:, q * width : (q + 1) * width] = jnp.dot(
-            sel_ref[q], tok_recv[...], preferred_element_type=f32
+            jnp.where(select, 1.0, 0.0).astype(bf16), tok_recv[...], preferred_element_type=f32
         )
 
     def normalize(x, gain):
@@ -113,18 +147,27 @@
     nrm[:ROWS] = normalize(x_ref[...], gain_ref[...]).astype(bf16)
     nrm[ROWS:] = normalize(own_ref[...].astype(f32), gain_ref[...]).astype(bf16)
 
-    rates = jnp.dot(nrm[:ROWS], wba_ref[...], preferred_element_type=f32)
+    rates = lax.dot_general(
+        nrm[:ROWS], wba_ref[...], (((1,), (1,)), ((), ())), preferred_element_type=f32
+    )
+    lane = lax.broadcasted_iota(jnp.int32, (1, 4 * HP), 1)
+    alog = jnp.zeros((1, 4 * HP), f32)
+    dtb = jnp.zeros((1, 4 * HP), f32)
+    for head in range(HV):
+        here = lane == 4 * (head // 2) + 2 + head % 2
+        alog = jnp.where(here, alog_ref[head], alog)
+        dtb = jnp.where(here, dtb_ref[head], dtb)
     write_rate = 1.0 / (1.0 + jnp.exp(-rates))
-    shifted = rates + dtb_ref[...]
+    shifted = rates + dtb
     softplus = jnp.maximum(shifted, 0.0) + jnp.log1p(jnp.exp(-jnp.abs(shifted)))
-    decays = jnp.exp(-jnp.exp(alog_ref[...]) * softplus)
+    decays = jnp.exp(-jnp.exp(alog) * softplus)
     request_of = lax.broadcasted_iota(jnp.int32, (2 * ROWS, 128), 0) % R
 
     loads[1].wait()
     for h in range(HP):
         projected = jnp.dot(nrm[...], wq[:, h * 768 : (h + 1) * 768], preferred_element_type=f32)
         rounded = projected[:, :512].astype(bf16)
-        ct_ref[:, h * 512 : (h + 1) * 512] = rounded[ROWS:]
+        ct_ref[:, h * 512 : (h + 1) * 512] = rounded[ROWS:].astype(f32)
         entered = rounded[:ROWS].astype(f32)
         window = [tails_ref[n][:, h * 512 : (h + 1) * 512] for n in range(3)]
         window += [entered[s * R : (s + 1) * R] for s in range(S)]
@@ -211,13 +254,14 @@
         for m in range(1, E):
             value = value + hp_recv[m - 1, q].astype(f32)
         res[q] = value
+        pgain[q] = pgain_ref[:, q * share : (q + 1) * share]
         square = square + jnp.sum(value * value, axis=-1, keepdims=True)
     scale = lax.rsqrt(square / D + epsilon)
 
     def rows_of(block):
         return pl.ds(pl.multiple_of(block * ROWS, ROWS), ROWS)
 
-    moe[e, rows_of(g)] = (res[e] * scale * pgain_ref[e]).astype(bf16)
+    moe[e, rows_of(g)] = (res[e] * scale * pgain[e]).astype(bf16)
 
     def group_copy(k):
         place = moe.at[e, rows_of(g)]
@@ -294,9 +338,11 @@
     lax.fori_loop(0, G, regroup, 0)
 
     lax.fori_loop(1, G, lambda k, c: (wts_copy(k).wait(), c)[1], 0)
-    picked = lax.broadcasted_iota(jnp.int32, (ROWS, 128), 0) == lax.broadcasted_iota(
-        jnp.int32, (ROWS, 128), 1
-    )
+    row = lax.broadcasted_iota(jnp.int32, (ROWS, 128), 0)
+    wanted = row // R
+    for i in range(R):
+        wanted = wanted + jnp.where(row % R == i, request_at[i] * S, 0)
+    picked = wanted == lax.broadcasted_iota(jnp.int32, (ROWS, 128), 1)
     for q in range(E):
         for l in range(L):
             out = jnp.dot(hid[l], dn[l, :, q * share : (q + 1) * share], preferred_element_type=f32)
@@ -352,25 +398,10 @@
     finish(ck_copies)
     finish(st_copies)
 
-    def put(i):
-        return pltpu.make_async_copy(st_new.at[i], st_out.at[i], out_sem.at[i])
-
-    def renew(i, carry):
-        for hv in range(HV):
-            h = hv // 2
-            k4 = ck_recv[i, S * HV + h * S : S * HV + (h + 1) * S]
-            c4 = ck_recv[i, hv * S : (hv + 1) * S]
-            row = S * HV + S * HP + hv
-            change = lax.dot_general(k4, c4, (((0,), (0,)), ((), ())), preferred_element_type=f32)
-            st_new[i, hv] = ck_recv[i, row : row + 1] * st_recv[i, hv].astype(f32) + change
-        put(i).start()
-        return carry
-
-    lax.fori_loop(0, R, renew, 0)
     for k in range(1, G):
         z_copy(k).wait_recv()
         final = final + z_recv[k].astype(f32)
-    lay_ref[...] = final.astype(bf16)
+    lay_ref[...] = final
 
     def drain(k, carry):
         group_copy(k).wait_send()
@@ -386,7 +417,6 @@
         return carry
 
     lax.fori_loop(0, G, drain_ep, 0)
-    lax.fori_loop(0, R, lambda i, c: (put(i).wait(), c)[1], 0)
 
 
 def body(
@@ -410,58 +440,33 @@
         which * stride if stride == 1 or which == R // 2 else (which * stride - 1) % G
         for which in range(R)
     ]
-    offset_array = jnp.array(offsets, jnp.int32)
-    slot_offsets = (src_group[0] % G).astype(jnp.int32)
-    matches = (slot_offsets[:, None] == offset_array[None, :]).astype(jnp.int32)
-    request_at = jnp.argmax(matches, axis=0)
-    place_of = jnp.argmax(matches, axis=1)
-    slots = src_slot[(g - offset_array) % G, request_at].astype(jnp.int32)
-
-    parts = 16 // S
-    ordered = tokens.reshape(R, S, D)[request_at]
-    tok = ordered.reshape(R * 16, D // parts)
-    rows = jnp.arange(ROWS)
-    source = (rows % R) * 16 + (rows // R) * parts
-    sel = (
-        (source[None, :, None] + jnp.arange(parts)[:, None, None]) == jnp.arange(R * 16)[None, None, :]
-    ).astype(bf16)
-
-    expert_of = (jnp.arange(G)[:, None] * E + e) * L + jnp.arange(L)[None, :]
-    hits = expert_ids[None, None] == expert_of[:, :, None, None]
-    dense = jnp.sum(jnp.where(hits, gate_probs[None, None], 0.0), axis=-1)
-    dense = dense.reshape(G, L, R, S)[:, :, request_at].transpose(0, 1, 3, 2).reshape(G, L, ROWS)
-    wts = jnp.pad(dense, ((0, 0), (0, 8 - L), (0, 128 - ROWS)))
-
-    tails = prefill_tails[slots].transpose(1, 0, 2).astype(f32)
-    zero = jnp.zeros((HP, 2), f32)
-    alog = jnp.concatenate([zero, a_log.reshape(HP, 2)], axis=1).reshape(1, 4 * HP)
-    dtb = jnp.concatenate([zero, dt_bias.reshape(HP, 2)], axis=1).reshape(1, 4 * HP)
-
     ck_rows = -(-(S * HV + S * HP + HV) // 8) * 8
     vm = pl.BlockSpec(memory_space=pltpu.VMEM)
     anywhere = pl.BlockSpec(memory_space=pl.ANY)
     dma = pltpu.SemaphoreType.DMA
     V = pltpu.VMEM
-    layer, conv_rows, states = pl.pallas_call(
+    layer, conv_rows, arrived, change = pl.pallas_call(
         functools.partial(kernel, G, E, tuple(offsets), S),
         out_shape=(
-            jax.ShapeDtypeStruct((ROWS, share), bf16),
-            jax.ShapeDtypeStruct((ROWS, C), bf16),
-            jax.ShapeDtypeStruct(prefill_states.shape, f32),
+            jax.ShapeDtypeStruct((ROWS, share), f32),
+            jax.ShapeDtypeStruct((ROWS, C), f32),
+            jax.ShapeDtypeStruct(prefill_states.shape, bf16),
+            jax.ShapeDtypeStruct((R, ck_rows, 128), f32),
         ),
-        in_specs=[pl.BlockSpec(memory_space=pltpu.SMEM)] + [vm] * 12 + [anywhere] * 5,
-        out_specs=(vm, vm, anywhere),
+        in_specs=[pl.BlockSpec(memory_space=pltpu.SMEM)] * 4 + [vm] * 9 + [anywhere] * 5,
+        out_specs=(vm, vm, anywhere, anywhere),
         scratch_shapes=[
             V(w_qkvz.shape, bf16), V(w_out.shape, bf16), V(gate_up_weight.shape, bf16),
             V(down_weight.shape, bf16), V(prefill_states.shape, f32),
-            V(prefill_states.shape, bf16), V(prefill_states.shape, bf16), V(prefill_states.shape, f32),
-            V(tok.shape, bf16), V((G, 8, 128), f32), V((ROWS, D), f32), V((2 * ROWS, D), bf16),
-            V((ROWS, HV * 128), f32), V((R, ck_rows, 128), f32), V((R, ck_rows, 128), f32),
+            V(prefill_states.shape, bf16), V((R, 8, D), f32), V((16 * R, S * D // 16), bf16),
+            V((3, R, C), f32), V((G, 8, 128), f32), V((16 * R, S * D // 16), bf16), V((G, 8, 128), f32), V((ROWS, D), f32), V((2 * ROWS, D), bf16),
+            V((ROWS, HV * 128), f32), V((R, ck_rows, 128), f32),
             V((E, ROWS, share), bf16), V((E - 1, E, ROWS, share), bf16), V((E, ROWS, share), f32),
+            V((E, 1, share), f32),
             V((E, G * ROWS, share), bf16), V((L, G * ROWS, F), f32), V((L, G * ROWS, F), bf16),
             V((E, G * ROWS, share), bf16), V((E - 1, G * ROWS, share), bf16),
             V((G, ROWS, share), f32), V((G, ROWS, share), bf16), V((G, ROWS, share), bf16),
-            dma((5,)), dma((R,)), dma((R,)), dma((R,)), dma((R,)), dma((R,)), dma((R,)), dma((R,)),
+            dma((5,)), dma((R,)), dma((R,)), dma((R,)), dma((R,)), dma((R,)), dma((R,)),
             dma((G,)), dma((G,)), dma((E - 1,)), dma((E - 1,)), dma((G,)), dma((G,)),
             dma((E - 1, G)), dma((E - 1, G)), dma((E - 1, G)), dma((E - 1, G)), dma((G,)), dma((G,)),
         ],
@@ -469,13 +474,67 @@
             collective_id=0, has_side_effects=True, vmem_limit_bytes=58 * 2**20
         ),
     )(
-        slots, tok, tokens, wts, tails, in_gain.reshape(1, D), w_ba, conv_weight, alog, dtb,
-        norm_gain.reshape(1, 128), post_gain.reshape(E, 1, share), sel,
-        w_qkvz, w_out, gate_up_weight, down_weight, prefill_states,
+        src_group, src_slot, a_log, dt_bias, tokens, expert_ids, gate_probs, prefill_tails,
+        in_gain.reshape(1, D), w_ba.T, conv_weight, norm_gain.reshape(1, 128),
+        post_gain.reshape(1, D), w_qkvz, w_out, gate_up_weight, down_weight, prefill_states,
     )
-    layer_out = layer.reshape(S, R, share)[:, place_of].transpose(1, 0, 2).reshape(ROWS, share)
-    new_tails = conv_rows.reshape(R, S, C)[:, S - 3 :]
-    return (layer_out, states[place_of], new_tails)
+
+    def place(j, table):
+        found = jnp.int32(0)
+        for i, offset in enumerate(offsets):
+            found = jnp.where(table[0, j] == offset, i, found)
+        return found
+
+    whole = lambda shape: pl.BlockSpec(shape, lambda j, table: (0,) * len(shape))
+    layer_out, new_states, new_tails = pl.pallas_call(
+        functools.partial(renew, place, S),
+        out_shape=(
+            jax.ShapeDtypeStruct((ROWS, share), bf16),
+            jax.ShapeDtypeStruct(prefill_states.shape, f32),
+            jax.ShapeDtypeStruct((R, 3, C), bf16),
+        ),
+        grid_spec=pltpu.PrefetchScalarGridSpec(
+            num_scalar_prefetch=1,
+            grid=(R,),
+            in_specs=[
+                whole((ROWS, share)),
+                whole((ROWS, C)),
+                pl.BlockSpec((1, HV, 128, 128), lambda j, table: (place(j, table), 0, 0, 0)),
+                pl.BlockSpec((1, ck_rows, 128), lambda j, table: (place(j, table), 0, 0)),
+            ],
+            out_specs=(
+                whole((ROWS, share)),
+                pl.BlockSpec((1, HV, 128, 128), lambda j, table: (j, 0, 0, 0)),
+                whole((R, 3, C)),
+            ),
+            scratch_shapes=[V((ROWS, share), f32)],
+        ),
+        compiler_params=pltpu.CompilerParams(vmem_limit_bytes=56 * 2**20),
+    )(src_group, layer, conv_rows, arrived, change)
+    return (layer_out, new_states, new_tails)
+
+
+def renew(place, S, table, lay_ref, ct_ref, st_ref, ck_ref, lay_out, st_out, tail_out, ordered):
+    R = tail_out.shape[0]
+    HV = st_ref.shape[1]
+    HP = HV // 2
+
+    @pl.when(pl.program_id(0) == 0)
+    def rows():
+        for j in range(R):
+            i = place(j, table)
+            for s in range(S):
+                ordered[j * S + s : j * S + s + 1, :] = lay_ref[pl.ds(s * R + i, 1), :]
+            tail_out[j] = ct_ref[(j + 1) * S - 3 : (j + 1) * S, :].astype(bf16)
+        lay_out[...] = ordered[...].astype(bf16)
+
+    for hv in range(HV):
+        h = hv // 2
+        k4 = ck_ref[0, S * HV + h * S : S * HV + (h + 1) * S]
+        c4 = ck_ref[0, hv * S : (hv + 1) * S]
+        row = S * HV + S * HP + hv
+        change = lax.dot_general(k4, c4, (((0,), (0,)), ((), ())), preferred_element_type=f32)
+        st_out[0, hv] = ck_ref[0, row : row + 1] * st_ref[0, hv].astype(f32) + change
 
 
 def solution(mesh):

time: 119 us -> 109 us (0.916); the launches traced: 119 us -> 107 us
  local copies, waits for them, and re-layouts: 18.5 us -> 6.01 us
  Pallas kernels: 95.3 us -> 101 us
  other arithmetic: 4.26 us -> 0 us
    gather x6 -> x0, local copies, waits for them, and re-layouts: 9.04 us -> none  [the longest x1 5.05 us: body(): return (layer_out, states[place_of], new_tails)]
    pallas_call x0 -> x1, Pallas kernels: none -> 8.18 us  [body(): pl.pallas_call(functools.partial(renew, place, S), out_shape=(jax.ShapeDt...]
    reshape x10 -> x0, local copies, waits for them, and re-layouts: 5.88 us -> none  [the longest x2 1.4 us: body(): layer.reshape(S, R, share)[:, place_of].transpose(1, 0, 2)]
    pallas_call x1, Pallas kernels: 95.3 us -> 92.5 us  [body(): pl.pallas_call(functools.partial(kernel, G, E, tuple(offsets), S), out_sh...]
    unnamed x8 -> x3, local copies, waits for them, and re-layouts: 2.58 us -> 4.39 us
    pallas_call x0 -> x1, local copies, waits for them, and re-layouts: none -> 1.62 us  [body(): pl.pallas_call(functools.partial(renew, place, S), out_shape=(jax.ShapeDt...]
    convert_element_type x2 -> x0, other arithmetic: 1.38 us -> none  [the longest x1 0.7 us: body(): sel = (source[None, :, None] + jnp.arange(parts)[:, None, None] == jnp.ar...]
    another operation x2 -> x0, other arithmetic: 1.29 us -> none  [the longest x1 0.7 us: body(): place_of = jnp.argmax(matches, axis=1)]
where the time goes in v3:
time: 109 us; the launch traced here: 107 us
  Pallas kernels  101 us (93%)
  local copies, waits for them, and re-layouts  6.01 us (6%)
    pallas_call x1, Pallas kernels, body(): pl.pallas_call(functools.partial(kernel, G, E, tuple(offsets), S), out_sh...  92.5 us
    pallas_call x1, Pallas kernels, body(): pl.pallas_call(functools.partial(renew, place, S), out_shape=(jax.ShapeDt...  8.18 us
    unnamed x3, local copies, waits for them, and re-layouts  4.39 us

profile of v3, /device:TPU:0, one launch (start us, length us, event | category | flops | bytes accessed | tf_op | source)
XLA Modules:
  0.0 107.4 jit_solution(8471024175538882331)
XLA Ops:
  0.6 1.4 %copy.21.ids_ref = s32[32,10]{1,0:T(8,128)} copy(s32[32,10]{0,1:T(8,128)} %param.32) | data formatting | bytes 2560 | tf_op args[14]
  2.0 1.4 %copy.22.probs_ref = f32[32,10]{1,0:T(8,128)} copy(f32[32,10]{0,1:T(8,128)} %param.33) | data formatting | bytes 2560 | tf_op args[15]
  3.4 1.6 %copy.23.tail_ref = bf16[8,3,2048]{2,1,0:T(4,128)(2,1)} copy(bf16[8,3,2048]{2,0,1:T(8,128)(2,1)} %param.20) | data formatting | bytes 196608 | tf_op args[2]
  5.0 92.5 %shard_map.193 = (f32[32,512]{1,0:T(8,128)}, f32[32,2048]{1,0:T(8,128)}, bf16[8,8,128,128]{3,2,1,0:T(8,128)(2,1)}, f32[8,56,128]{2,1,0:T(8,128)}) custom-call(s32[8,8]{1,0:T(8,128)} %table.1, s32[8,8]{1,0:T(8,128)} %sslot_ref.1, f32[8]{0:T(128)} %alog_ref.1, f32[8]{0:T(128)} %dtb_ref.1, bf16[32,2048]{1,0:T(8,128)(2,1)} %own_ref.1, s32[32,10]{1,0:T(8,128)} %copy.21.ids_ref, ...), custom_call_target="tpu_custom_call" | custom-call | tf_op jit(solution)/shard_map/pallas_call | solution.py:448
  97.6 8.2 %shard_map.194 = (bf16[32,512]{1,0:T(8,128)(2,1)}, f32[8,8,128,128]{3,2,1,0:T(8,128)}, bf16[8,3,2048]{2,1,0:T(4,128)(2,1)}) custom-call(s32[8,8]{1,0:T(8,128)} %table.1, f32[32,512]{1,0:T(8,128)} %get-tuple-element.7.lay_ref, f32[32,2048]{1,0:T(8,128)} %get-tuple-element.8.ct_ref, bf16[8,8,128,128]{3,2,1,0:T(8,128)(2,1)} %get-tuple-element.9.st_ref, ...), custom_call_target="tpu_custom_call" | custom-call | tf_op jit(solution)/shard_map/pallas_call | solution.py:489
  105.8 1.6 %copy.24 = bf16[8,3,2048]{2,0,1:T(8,128)(2,1)} copy(bf16[8,3,2048]{2,1,0:T(4,128)(2,1)} %get-tuple-element.13) | data formatting | bytes 196608 | tf_op jit(solution)/shard_map/pallas_call | solution.py:489

commit v4 on v3

--- a/solution.py
+++ b/solution.py
@@ -20,7 +20,7 @@
     sgroup_ref, sslot_ref, alog_ref, dtb_ref, own_ref, ids_ref, probs_ref, tail_ref, gain_ref, wba_ref,
     conv_ref, ngain_ref, pgain_ref, wq_hbm, wo_hbm, gu_hbm, dn_hbm, st_hbm,
     lay_ref, ct_ref, st_recv, ck_recv,
-    wq, wo, gu, dn, st, st_send, own32, tok_ref, tails_ref, wts_ref, tok_recv, wts_all, x_ref, nrm,
+    wq, wo, gu, dn, st, st_send, own32, tok_ref, tails32, tails_ref, wts_ref, tok_recv, wts_all, x_ref, nrm,
     gated, ck_send, hp_send, hp_recv, res, pgain, moe, hidden, hid, y_send, y_recv, base, part, z_recv,
     load_sem, tok_ss, tok_rs, st_ss, st_rs, ck_ss, ck_rs, w_ss, w_rs,
     hp_ss, hp_rs, g_ss, g_rs, e_ss, e_rs, y_ss, y_rs, z_ss, z_rs,
@@ -45,6 +45,18 @@
     for copy in loads:
         copy.start()
 
+    barrier = pltpu.get_barrier_semaphore()
+
+    def greet_group(k, carry):
+        pl.semaphore_signal(barrier, inc=1, device_id=(lax.rem(g + k, G), e), device_id_type=MESH)
+        return carry
+
+    def greet_ep(m, carry):
+        pl.semaphore_signal(barrier, inc=1, device_id=(g, lax.rem(e + m, E)), device_id_type=MESH)
+        return carry
+
+    lax.fori_loop(1, G, greet_group, 0)
+    lax.fori_loop(1, E, greet_ep, 0)
     asked = [sgroup_ref[0, j] for j in range(R)]
     request_at = []
     for offset in offsets:
@@ -55,6 +67,7 @@
     slots = [sslot_ref[lax.rem(g + G - offsets[i], G), request_at[i]] for i in range(R)]
     quarter = 16 // S
     width = D // quarter
+    tails32[...] = tail_ref[...].astype(f32)
     own = own_ref[...].astype(f32)
     for j in range(R):
         own32[j, :S, :] = own[j * S : (j + 1) * S]
@@ -63,33 +76,16 @@
         tok_ref[16 * i : 16 * (i + 1), :] = jnp.concatenate(
             [four[:, q * width : (q + 1) * width] for q in range(quarter)], axis=0
         ).astype(bf16)
-        tail = tail_ref[slots[i]].astype(f32)
         for n in range(3):
-            tails_ref[n, i : i + 1, :] = tail[n : n + 1]
-    diagonal = lax.broadcasted_iota(jnp.int32, (ROWS, 128), 0) == lax.broadcasted_iota(
-        jnp.int32, (ROWS, 128), 1
-    )
+            tails_ref[n, i : i + 1, :] = tails32[n, pl.ds(slots[i], 1), :]
     wts_ref[...] = jnp.zeros_like(wts_ref)
     for to in range(G):
         for l in range(L):
             named = ids_ref[...] == (to * E + e) * L + l
-            weight = jnp.sum(jnp.where(named, probs_ref[...], 0.0), axis=-1, keepdims=True)
-            wts_ref[to, l : l + 1, :] = jnp.sum(
-                jnp.where(diagonal, weight, 0.0), axis=0, keepdims=True
+            wts_ref[to, l : l + 1, :ROWS] = jnp.sum(
+                jnp.where(named, probs_ref[...], 0.0), axis=0, keepdims=True
             )
 
-    barrier = pltpu.get_barrier_semaphore()
-
-    def greet_group(k, carry):
-        pl.semaphore_signal(barrier, inc=1, device_id=(lax.rem(g + k, G), e), device_id_type=MESH)
-        return carry
-
-    def greet_ep(m, carry):
-        pl.semaphore_signal(barrier, inc=1, device_id=(g, lax.rem(e + m, E)), device_id_type=MESH)
-        return carry
-
-    lax.fori_loop(1, G, greet_group, 0)
-    lax.fori_loop(1, E, greet_ep, 0)
     pl.semaphore_wait(barrier, G - 1 + E - 1)
 
     def move(src, dst, ss, rs, i, group):
@@ -459,7 +455,7 @@
             V(w_qkvz.shape, bf16), V(w_out.shape, bf16), V(gate_up_weight.shape, bf16),
             V(down_weight.shape, bf16), V(prefill_states.shape, f32),
             V(prefill_states.shape, bf16), V((R, 8, D), f32), V((16 * R, S * D // 16), bf16),
-            V((3, R, C), f32), V((G, 8, 128), f32), V((16 * R, S * D // 16), bf16), V((G, 8, 128), f32), V((ROWS, D), f32), V((2 * ROWS, D), bf16),
+            V((3, R, C), f32), V((3, R, C), f32), V((G, 8, 128), f32), V((16 * R, S * D // 16), bf16), V((G, 8, 128), f32), V((ROWS, D), f32), V((2 * ROWS, D), bf16),
             V((ROWS, HV * 128), f32), V((R, ck_rows, 128), f32),
             V((E, ROWS, share), bf16), V((E - 1, E, ROWS, share), bf16), V((E, ROWS, share), f32),
             V((E, 1, share), f32),
@@ -474,7 +470,8 @@
             collective_id=0, has_side_effects=True, vmem_limit_bytes=58 * 2**20
         ),
     )(
-        src_group, src_slot, a_log, dt_bias, tokens, expert_ids, gate_probs, prefill_tails,
+        src_group, src_slot, a_log, dt_bias, tokens, expert_ids.T, gate_probs.T,
+        prefill_tails.transpose(1, 0, 2),
         in_gain.reshape(1, D), w_ba.T, conv_weight, norm_gain.reshape(1, 128),
         post_gain.reshape(1, D), w_qkvz, w_out, gate_up_weight, down_weight, prefill_states,
     )
@@ -491,7 +488,7 @@
         out_shape=(
             jax.ShapeDtypeStruct((ROWS, share), bf16),
             jax.ShapeDtypeStruct(prefill_states.shape, f32),
-            jax.ShapeDtypeStruct((R, 3, C), bf16),
+            jax.ShapeDtypeStruct((3, R, C), bf16),
         ),
         grid_spec=pltpu.PrefetchScalarGridSpec(
             num_scalar_prefetch=1,
@@ -505,17 +502,17 @@
             out_specs=(
                 whole((ROWS, share)),
                 pl.BlockSpec((1, HV, 128, 128), lambda j, table: (j, 0, 0, 0)),
-                whole((R, 3, C)),
+                whole((3, R, C)),
             ),
-            scratch_shapes=[V((ROWS, share), f32)],
+            scratch_shapes=[V((ROWS, share), f32), V((3, R, C), f32)],
         ),
         compiler_params=pltpu.CompilerParams(vmem_limit_bytes=56 * 2**20),
     )(src_group, layer, conv_rows, arrived, change)
-    return (layer_out, new_states, new_tails)
-
-
-def renew(place, S, table, lay_ref, ct_ref, st_ref, ck_ref, lay_out, st_out, tail_out, ordered):
-    R = tail_out.shape[0]
+    return (layer_out, new_states, new_tails.transpose(1, 0, 2))
+
+
+def renew(place, S, table, lay_ref, ct_ref, st_ref, ck_ref, lay_out, st_out, tail_out, ordered, last):
+    R = tail_out.shape[1]
     HV = st_ref.shape[1]
     HP = HV // 2
 
@@ -525,7 +522,10 @@
             i = place(j, table)
             for s in range(S):
                 ordered[j * S + s : j * S + s + 1, :] = lay_ref[pl.ds(s * R + i, 1), :]
-            tail_out[j] = ct_ref[(j + 1) * S - 3 : (j + 1) * S, :].astype(bf16)
+            for n in range(3):
+                row = (j + 1) * S - 3 + n
+                last[n, j : j + 1, :] = ct_ref[row : row + 1, :]
+        tail_out[...] = last[...].astype(bf16)
         lay_out[...] = ordered[...].astype(bf16)
 
     for hv in range(HV):

time: 109 us -> 103 us (0.945)
  local copies, waits for them, and re-layouts: 6.01 us -> 0 us
    unnamed x3 -> x0, local copies, waits for them, and re-layouts: 4.39 us -> none
    pallas_call x1 -> x0, local copies, waits for them, and re-layouts: 1.62 us -> none  [body(): pl.pallas_call(functools.partial(renew, place, S), out_shape=(jax.ShapeDt...]
where the time goes in v4:
time: 103 us; the launch traced here: 101 us
  Pallas kernels  101 us (98%)
    pallas_call x1, Pallas kernels, body(): pl.pallas_call(functools.partial(kernel, G, E, tuple(offsets), S), out_sh...  92.3 us
    pallas_call x1, Pallas kernels, body(): pl.pallas_call(functools.partial(renew, place, S), out_shape=(jax.ShapeDt...  8.21 us

profile of v4, /device:TPU:0, one launch (start us, length us, event | category | flops | bytes accessed | tf_op | source)
XLA Modules:
  0.0 101.2 jit_solution(14118493445606365102)
XLA Ops:
  0.6 92.3 %shard_map.193 = (f32[32,512]{1,0:T(8,128)}, f32[32,2048]{1,0:T(8,128)}, bf16[8,8,128,128]{3,2,1,0:T(8,128)(2,1)}, f32[8,56,128]{2,1,0:T(8,128)}) custom-call(s32[8,8]{1,0:T(8,128)} %table.1, s32[8,8]{1,0:T(8,128)} %sslot_ref.1, f32[8]{0:T(128)} %alog_ref.1, f32[8]{0:T(128)} %dtb_ref.1, bf16[32,2048]{1,0:T(8,128)(2,1)} %own_ref.1, s32[10,32]{1,0:T(8,128)} %bitcast.10, ...), custom_call_target="tpu_custom_call" | custom-call | tf_op jit(solution)/shard_map/pallas_call | solution.py:444
  92.9 8.2 %shard_map.194 = (bf16[32,512]{1,0:T(8,128)(2,1)}, f32[8,8,128,128]{3,2,1,0:T(8,128)}, bf16[3,8,2048]{2,1,0:T(8,128)(2,1)}) custom-call(s32[8,8]{1,0:T(8,128)} %table.1, f32[32,512]{1,0:T(8,128)} %get-tuple-element.10.lay_ref, f32[32,2048]{1,0:T(8,128)} %get-tuple-element.11.ct_ref, bf16[8,8,128,128]{3,2,1,0:T(8,128)(2,1)} %get-tuple-element.12.st_ref, ...), custom_call_target="tpu_custom_call" | custom-call | tf_op jit(solution)/shard_map/pallas_call | solution.py:486
